TPU v7x, 32 devices: a whole 2x2x4 slice. The times are simulated.
32 devices in a mesh: dp: 4 (over y, x), expert: 8 (over z, core).
Axes of the slice: x: 2, y: 2, z: 4, core: 2. Of those that a mesh axis runs over, the one named last changes fastest.
Arguments:
- tokens: bfloat16 [8, 88, 4096], P('expert'), may hold values from -6 to 6
- routing: int32 [8, 88, 8], P('expert'), may hold values from 0 to 63, as said below
- combine: float32 [8, 88, 8], P('expert'), may hold values from 0.05 to 0.5
- w_gate: bfloat16 [64, 4096, 1536], P('expert', None, 'dp'), may hold values from -0.09375 to 0.09375
- w_up: bfloat16 [64, 4096, 1536], P('expert', None, 'dp'), may hold values from -0.09375 to 0.09375
- w_down: bfloat16 [64, 1536, 4096], P('expert', 'dp'), may hold values from -0.15625 to 0.15625
Outputs:
- mixed: bfloat16 [8, 88, 4096], P('expert', None, 'dp')
Inputs may be any that keep to these rules, and one draw needn't show every extreme that they name: `routing`: each token names 8 different experts. In every group one expert, the same in all groups, is chosen by exactly 44 tokens; every other expert is chosen by 5 to 13 tokens of a group, and one of them, the same in all groups, by exactly 13 tokens of every group.
All inputs are finite; a program needn't handle non-finite values.
Results may differ from a plain program's by a relative error of at most 0.015.
Values may be sent and summed in bfloat16 or wider, within the bound.
No kernel may reach another device: no remote copies, remote signals or barrier semaphores. Data moves between devices by JAX's collectives and lax.ppermute only.
A program may use at most 192 MiB of HBM per device.

v0:
```python
import jax
import jax.numpy as jnp
from jax import lax
from jax.sharding import PartitionSpec as P

CAP = 13
HOT_CAP = 44


def broadcast(block, axis, holder):
    block = jnp.where(lax.axis_index(axis) == holder, block, jnp.zeros_like(block))
    return lax.psum(block, axis)


def expert_partial(inputs, gate_mat, up_mat, down_mat):
    gate_val = jnp.dot(inputs, gate_mat, preferred_element_type=jnp.float32)
    up_val = jnp.dot(inputs, up_mat, preferred_element_type=jnp.float32)
    hidden = (jax.nn.silu(gate_val) * up_val).astype(jnp.bfloat16)
    return jnp.dot(hidden, down_mat, preferred_element_type=jnp.float32)


def local(tokens, routing, combine, w_gate, w_up, w_down):
    group_rows = tokens[0]
    chosen = routing[0]
    mixing = combine[0]
    owners = lax.axis_size("expert")
    local_experts = w_gate.shape[0]
    experts = owners * local_experts
    group_tok, top_k = chosen.shape
    model_width = group_rows.shape[1]
    capacity = CAP
    hot_capacity = HOT_CAP
    pick_ids = chosen.reshape(-1)
    one_hot = (pick_ids[:, None] == jnp.arange(experts, dtype=jnp.int32)[None, :]).astype(jnp.int32)
    counts = jnp.sum(one_hot, axis=0)
    hot_expert = jnp.argmax(counts)
    slot_rank = jnp.sum((jnp.cumsum(one_hot, axis=0) - 1) * one_hot, axis=1)
    is_hot = pick_ids == hot_expert
    token_of = jnp.arange(pick_ids.shape[0], dtype=jnp.int32) // top_k
    cold_slot = jnp.where(is_hot, experts * capacity, pick_ids * capacity + slot_rank)
    slot_token = (
        jnp.full((experts * capacity,), group_tok, jnp.int32)
        .at[cold_slot]
        .set(token_of, mode="drop")
    )
    hot_slot = jnp.where(is_hot, slot_rank, hot_capacity)
    hot_token = (
        jnp.full((hot_capacity,), group_tok, jnp.int32).at[hot_slot].set(token_of, mode="drop")
    )
    padded = jnp.concatenate([group_rows, jnp.zeros((1, model_width), group_rows.dtype)], axis=0)
    outgoing = jnp.take(padded, slot_token, axis=0).reshape(
        owners, local_experts, capacity, model_width
    )
    local_pick = hot_expert % local_experts
    owner_index = hot_expert // local_experts
    own_gate = lax.dynamic_index_in_dim(w_gate, local_pick, 0, keepdims=False)
    own_up = lax.dynamic_index_in_dim(w_up, local_pick, 0, keepdims=False)
    own_down = lax.dynamic_index_in_dim(w_down, local_pick, 0, keepdims=False)
    hot_gate, hot_up, hot_down = (
        broadcast(own_gate, "expert", owner_index),
        broadcast(own_up, "expert", owner_index),
        broadcast(own_down, "expert", owner_index),
    )
    hot_partial = expert_partial(jnp.take(padded, hot_token, axis=0), hot_gate, hot_up, hot_down)
    received = lax.all_to_all(outgoing, "expert", split_axis=0, concat_axis=0, tiled=True)
    gate_val = jnp.einsum("senm,emf->senf", received, w_gate, preferred_element_type=jnp.float32)
    up_val = jnp.einsum("senm,emf->senf", received, w_up, preferred_element_type=jnp.float32)
    hidden = (jax.nn.silu(gate_val) * up_val).astype(jnp.bfloat16)
    partial_value = jnp.einsum("senf,efm->senm", hidden, w_down, preferred_element_type=jnp.float32)
    returned = lax.all_to_all(
        partial_value.astype(jnp.bfloat16), "expert", split_axis=0, concat_axis=0, tiled=True
    )
    flat_back = returned.reshape(experts * capacity, returned.shape[3])
    cold_sum, hot_sum = (
        lax.psum_scatter(flat_back, "dp", scatter_dimension=1, tiled=True).astype(jnp.float32),
        lax.psum_scatter(
            hot_partial.astype(jnp.bfloat16), "dp", scatter_dimension=1, tiled=True
        ).astype(jnp.float32),
    )
    cold_share = cold_sum.astype(jnp.bfloat16)
    hot_share = hot_sum.astype(jnp.bfloat16)
    out_table = jnp.concatenate([cold_share, hot_share], axis=0)
    target = jnp.where(
        is_hot, experts * capacity + slot_rank, pick_ids * capacity + slot_rank
    ).reshape(group_tok, top_k)
    combined = jnp.zeros((group_tok, out_table.shape[1]), jnp.float32)
    for column in range(top_k):
        picked = jnp.take(out_table, target[:, column], axis=0).astype(jnp.float32)
        combined = combined + mixing[:, column : column + 1] * picked
    return combined.astype(jnp.bfloat16)[None]


def solution(mesh):
    placed = (
        P("expert", None, None),
        P("expert", None, None),
        P("expert", None, None),
        P("expert", None, "dp"),
        P("expert", None, "dp"),
        P("expert", "dp", None),
    )
    return jax.shard_map(
        local, mesh=mesh, in_specs=placed, out_specs=P("expert", None, "dp"), check_vma=False
    )
```

profile of v0, /device:TPU:0, one launch (start us, length us, event | category | flops | bytes accessed | tf_op | source)
XLA Modules:
  0.0 678.2 jit_solution(419473845554990469)
XLA Ops:
  8.3 1.8 reduce-window.6
  12.5 4.1 scatter_custom_fusion
  16.6 1.2 concatenate.6
  17.8 6.5 gather_fusion
  24.3 9.1 %gather.14 = bf16[8,8,13,4096]{3,2,1,0:T(8,128)(2,1)} reshape(bf16[832,4096]{1,0:T(8,128)(2,1)} %gather_fusion) | data formatting | bytes 13631488 | tf_op jit(solution)/shard_map/jit(_take)/gather | solution.py:51
  33.6 7.4 %broadcast_select_fusion = bf16[8,8,13,4096]{3,2,1,0:T(8,128)(2,1)} fusion(bf16[8,8,13,4096]{3,2,1,0:T(8,128)(2,1)} %gather.14, pred[8,8,13]{2,1,0:T(8,128)(4,1)S(1)} %broadcast_in_dim.63), kind=kLoop, calls=%fused_computation.19 | loop fusion | flops 3407872 | bytes 13632320 | tf_op jit(solution)/shard_map/jit(_take)/select_n | solution.py:51
  41.0 8.0 %copy.28 = bf16[8,8,13,4096]{3,1,2,0:T(8,128)(2,1)S(1)} copy(bf16[8,8,13,4096]{3,2,1,0:T(8,128)(2,1)} %broadcast_select_fusion) | data formatting | bytes 13631488 | tf_op jit(solution)/shard_map/jit(_take)/select_n | solution.py:51
  49.0 156.8 %all_to_all.10 = bf16[8,8,13,4096]{3,1,2,0:T(8,128)(2,1)} all-to-all(bf16[8,8,13,4096]{3,1,2,0:T(8,128)(2,1)S(1)} %copy.28), channel_id=1, replica_groups=mesh['dp'=4,'expert'=8] {'expert'}, dimensions={0} | all-to-all | bytes 13631488 | tf_op jit(solution)/shard_map/all_to_all | solution.py:65
  205.8 19.7 %fusion.2 = f32[8,8,13,384]{3,2,1,0:T(8,128)S(1)} fusion(bf16[8,4096,384]{2,1,0:T(8,128)(2,1)} %param.12, bf16[8,8,13,4096]{3,1,2,0:T(8,128)(2,1)} %all_to_all.10), kind=kOutput, calls=%fused_computation.14 | convolution fusion | flops 2617245696 | bytes 33259520 | tf_op jit(solution)/shard_map/senm,emf->senf/dot_general | solution.py:67
  225.5 51.7 %convert_bitcast_fusion = bf16[8,8,13,4096]{3,2,0,1:T(8,128)(2,1)} fusion(bf16[8,384,4096]{2,1,0:T(8,128)(2,1)} %param.13, f32[8,8,13,384]{3,2,1,0:T(8,128)S(1)} %fusion.2, bf16[8,4096,384]{2,1,0:T(8,128)(2,1)} %param.11, bf16[8,8,13,4096]{3,1,2,0:T(8,128)(2,1)} %all_to_all.10), kind=kOutput, calls=%fused_computation.18 | convolution fusion | flops 5239816192 | bytes 65241088 | tf_op jit(solution)/shard_map/senf,efm->senm/dot_general | solution.py:69
  277.2 10.9 %copy.31 = bf16[8,8,13,4096]{3,1,2,0:T(8,128)(2,1)} copy(bf16[8,8,13,4096]{3,2,0,1:T(8,128)(2,1)} %convert_bitcast_fusion) | data formatting | bytes 13631488 | tf_op jit(solution)/shard_map/convert_element_type | solution.py:71
  288.1 4.8 all-to-all-start.1
  296.0 3.7 select_bitcast_fusion
  299.7 6.0 select_bitcast_fusion.1
  305.8 201.1 %all-to-all-done.1 = bf16[8,8,13,4096]{3,1,2,0:T(8,128)(2,1)} async-done(((bf16[8,8,13,4096]{3,1,2,0:T(8,128)(2,1)}), bf16[8,8,13,4096]{3,1,2,0:T(8,128)(2,1)}, u32[]{:S(2)}, u32[]{:S(2)}) %all-to-all-start.1) | async-done | bytes 6815776 | tf_op jit(solution)/shard_map/all_to_all | solution.py:70
  506.9 10.9 %copy.32 = bf16[8,8,13,4096]{3,2,1,0:T(8,128)(2,1)} copy(bf16[8,8,13,4096]{3,1,2,0:T(8,128)(2,1)} %all-to-all-done.1) | data formatting | bytes 13631488 | tf_op jit(solution)/shard_map/all_to_all | solution.py:70
  517.8 9.4 %reshape.117 = bf16[832,4096]{1,0:T(8,128)(2,1)} reshape(bf16[8,8,13,4096]{3,2,1,0:T(8,128)(2,1)} %copy.32) | data formatting | bytes 13631488 | tf_op jit(solution)/shard_map/reshape | solution.py:73
  527.3 4.1 scatter_custom_fusion.1
  532.8 97.1 %all-reduce.5.cloned.1.call-done = (bf16[384,4096]{1,0:T(8,128)(2,1)}, bf16[4096,384]{1,0:T(8,128)(2,1)}, bf16[4096,384]{1,0:T(8,128)(2,1)}) async-done(((bf16[384,4096]{1,0:T(8,128)(2,1)}, bf16[4096,384]{1,0:T(8,128)(2,1)}, bf16[4096,384]{1,0:T(8,128)(2,1)}), (bf16[384,4096]{1,0:T(8,128)(2,1)}, bf16[4096,384]{1,0:T(8,128)(2,1)}, bf16[4096,384]{1,0:T(8,128)(2,1)})) %all-reduce.5.cloned.1.call-update) | async-done | bytes 9437200 | tf_op jit(solution)/shard_map/psum | solution.py:12
  629.9 2.5 fusion.27
  632.4 5.1 convolution_convert_fusion
  637.6 1.6 constant_dynamic-update-slice_fusion.1
  639.2 22.9 %reduce-scatter.5.cloned.1.call-done = bf16[44,1024]{1,0:T(8,128)(2,1)} async-done(((bf16[44,4096]{1,0:T(8,128)(2,1)}), bf16[44,1024]{1,0:T(8,128)(2,1)}) %reduce-scatter.5.cloned.1.call-update) | async-done | bytes 90128 | tf_op jit(solution)/shard_map/reduce_scatter | solution.py:76
  669.1 1.1 fusion.26
  (60 shorter events, 12.1 us)
Async XLA Ops:
  288.1 218.9 %all-to-all-start.1 = ((bf16[8,8,13,4096]{3,1,2,0:T(8,128)(2,1)}), bf16[8,8,13,4096]{3,1,2,0:T(8,128)(2,1)}, u32[]{:S(2)}, u32[]{:S(2)}) async-start(bf16[8,8,13,4096]{3,1,2,0:T(8,128)(2,1)} %copy.31), calls=%async_computation.1 | async-start | bytes 13631488 | tf_op jit(solution)/shard_map/all_to_all | solution.py:70
  292.9 337.0 %all-reduce.5.cloned.1.call-start = ((), (), s32[]{:S(2)}) async-start(), calls=%async_computation.6 | async-start | bytes 18874368 | tf_op jit(solution)/shard_map/psum | solution.py:12
  305.7 331.9 %reduce-scatter.3.cloned.1.call-start = ((), (), s32[]{:S(2)}) async-start(), calls=%async_computation.4 | async-start | bytes 8519680 | tf_op jit(solution)/shard_map/reduce_scatter | solution.py:75
  527.3 134.8 %reduce-scatter.5.cloned.1.call-start = ((), (), s32[]{:S(2)}) async-start(), calls=%async_computation.5 | async-start | bytes 491520 | tf_op jit(solution)/shard_map/reduce_scatter | solution.py:76
  632.4 5.2 copy-start
Sparse Core Ops, SparseCore 0:
  305.9 323.9 all-reduce.4
Sparse Core Ops, SparseCore 1:
  527.4 82.2 reduce-scatter.2
  637.6 24.5 reduce-scatter.4
where the time goes:
time: 686 us; the launch traced here: 678 us
  waiting for transfers between devices  321 us (47%)
  blocking collectives  157 us (23%)
  matrix products  79 us (12%)
  local copies, waits for them, and re-layouts  75.5 us (11%)
  other arithmetic  22 us (3%)
  between operations  18.4 us (3%)
    all_to_all x1, waiting for transfers between devices, local(): lax.all_to_all(partial_value.astype(jnp.bfloat16), 'expert', split_axis=0...  201 us
    all_to_all x1, blocking collectives, local(): lax.all_to_all(outgoing, 'expert', split_axis=0, concat_axis=0, tiled=True)  157 us
    psum x1, waiting for transfers between devices, broadcast(): return lax.psum(block, axis)  97.1 us
    dot_general x1, matrix products, local(): jnp.einsum('senf,efm->senm', hidden, w_down, preferred_element_type=jnp.f...  51.7 us
    reduce_scatter x1, waiting for transfers between devices, local(): lax.psum_scatter(hot_partial.astype(jnp.bfloat16), 'dp', scatter_dimensio...  22.9 us
    dot_general x1, matrix products, local(): jnp.einsum('senm,emf->senf', received, w_up, preferred_element_type=jnp.f...  19.7 us
    gather x2, local copies, waits for them, and re-layouts, local(): jnp.take(padded, slot_token, axis=0)  15.7 us
  transfers between devices with their start and end apart: 4, of which 3 were waited for; matrix products, arithmetic and copies ran while one was open for 7% of the time, Pallas kernels for 0%

commit v1 on v0

--- a/solution.py
+++ b/solution.py
@@ -1,10 +1,18 @@
+import functools
+
 import jax
 import jax.numpy as jnp
 from jax import lax
+from jax.experimental import pallas as pl
+from jax.experimental.pallas import tpu as pltpu
 from jax.sharding import PartitionSpec as P
 
 CAP = 13
 HOT_CAP = 44
+AXES = ("dp", "expert")
+BF16 = jnp.bfloat16
+F32 = jnp.float32
+VMEM_LIMIT = 56 * 1024 * 1024
 
 
 def broadcast(block, axis, holder):
@@ -19,7 +27,7 @@
     return jnp.dot(hidden, down_mat, preferred_element_type=jnp.float32)
 
 
-def local(tokens, routing, combine, w_gate, w_up, w_down):
+def dispatch_local(tokens, routing, combine, w_gate, w_up, w_down):
     group_rows = tokens[0]
     chosen = routing[0]
     mixing = combine[0]
@@ -90,6 +98,244 @@
     return combined.astype(jnp.bfloat16)[None]
 
 
+def gate_up_kernel(last, first, scal, onehot, hot_onehot, xa, xb, wg, wu, *rest):
+    rest = list(rest)
+    if not first:
+        acc_in, hacc_in = rest.pop(0), rest.pop(0)
+    if last:
+        scale, hscale = rest.pop(0), rest.pop(0)
+    out, hout, xg, xh = rest
+    e = pl.program_id(0)
+    half = xa.shape[0]
+    hot = scal[1]
+
+    def gather(table):
+        return (
+            jnp.dot(table[:, :half], xa[...], preferred_element_type=F32)
+            + jnp.dot(table[:, half:], xb[...], preferred_element_type=F32)
+        ).astype(BF16)
+
+    @pl.when(e == 0)
+    def _():
+        xg[...] = gather(onehot[...]).reshape(xg.shape)
+
+    def finish(g, u, scale_col):
+        return (g / (1.0 + jnp.exp(-g)) * u * scale_col).astype(BF16)
+
+    def work(x, prev, scale_col):
+        f = wg.shape[2]
+        g = jnp.dot(x, wg[0], preferred_element_type=F32)
+        u = jnp.dot(x, wu[0], preferred_element_type=F32)
+        if prev is not None:
+            g = g + prev[:, :f]
+            u = u + prev[:, f:]
+        if last:
+            return finish(g, u, scale_col)
+        return jnp.concatenate([g, u], axis=1)
+
+    out[0] = work(xg[e], None if first else acc_in[0], scale[0] if last else None)
+
+    @pl.when(e == hot)
+    def _():
+        xh[...] = gather(hot_onehot[...])
+        hout[...] = work(xh[...], None if first else hacc_in[...], hscale[...] if last else None)
+
+
+def gate_up(quarter, hot, onehot, hot_onehot, xa, xb, w_gate, w_up, acc, scales):
+    n, width, f = w_gate.shape
+    part = xa.shape[1]
+    rows = onehot.shape[0] // n
+    hrows = hot_onehot.shape[0]
+    first, last = acc is None, scales is not None
+    scal = jnp.stack([quarter, hot]).astype(jnp.int32)
+
+    def whole(a):
+        return pl.BlockSpec(a.shape, lambda e, s: (0,) * a.ndim)
+
+    def per_expert(*tail):
+        return pl.BlockSpec((1,) + tail, lambda e, s: (e,) + (0,) * len(tail))
+
+    w_spec = pl.BlockSpec((1, part, f), lambda e, s: (e, s[0], 0))
+    operands = [onehot, hot_onehot, xa, xb, w_gate, w_up]
+    specs = [whole(onehot), whole(hot_onehot), whole(xa), whole(xb), w_spec, w_spec]
+    if not first:
+        operands += list(acc)
+        specs += [per_expert(rows, 2 * f), whole(acc[1])]
+    if last:
+        operands += list(scales)
+        specs += [per_expert(rows, 1), whole(scales[1])]
+    if last:
+        outs = (jax.ShapeDtypeStruct((n, rows, f), BF16), jax.ShapeDtypeStruct((hrows, f), BF16))
+    else:
+        outs = (jax.ShapeDtypeStruct((n, rows, 2 * f), F32), jax.ShapeDtypeStruct((hrows, 2 * f), F32))
+    return pl.pallas_call(
+        functools.partial(gate_up_kernel, last, first),
+        grid_spec=pltpu.PrefetchScalarGridSpec(
+            num_scalar_prefetch=1,
+            grid=(n,),
+            in_specs=specs,
+            out_specs=(per_expert(*outs[0].shape[1:]), pl.BlockSpec(outs[1].shape, lambda e, s: (0, 0))),
+            scratch_shapes=[pltpu.VMEM((n, rows, part), BF16), pltpu.VMEM((hrows, part), BF16)],
+        ),
+        out_shape=outs,
+        compiler_params=pltpu.CompilerParams(vmem_limit_bytes=VMEM_LIMIT),
+        cost_estimate=pl.CostEstimate(
+            flops=4 * n * rows * part * f + 4 * n * rows * xa.shape[0] * part,
+            bytes_accessed=4 * n * part * f + 4 * xa.size,
+            transcendentals=0,
+        ),
+        name="gate_up",
+    )(scal, *operands)
+
+
+def down_kernel(scal, spread, hot_spread, hidden, hhidden, wd, out_a, out_b, y, yh):
+    e = pl.program_id(0)
+    hot = scal[1]
+    rows = hidden.shape[1]
+    half = out_a.shape[0]
+    at = pl.multiple_of(e * rows, 16)
+    y[pl.ds(at, rows), :] = jnp.dot(hidden[0], wd[0], preferred_element_type=F32).astype(BF16)
+
+    @pl.when(e == hot)
+    def _():
+        yh[...] = jnp.dot(hhidden[...], wd[0], preferred_element_type=F32).astype(BF16)
+
+    last = e == pl.num_programs(0) - 1
+
+    @pl.when(last & (hot < 0))
+    def _():
+        total = jnp.dot(spread[...], y[...], preferred_element_type=F32).astype(BF16)
+        out_a[...] = total[:half]
+        out_b[...] = total[half:]
+
+    @pl.when(last & (hot >= 0))
+    def _():
+        total = jnp.dot(spread[...], y[...], preferred_element_type=F32)
+        total = total + jnp.dot(hot_spread[...], yh[...], preferred_element_type=F32)
+        total = total.astype(BF16)
+        out_a[...] = total[:half]
+        out_b[...] = total[half:]
+
+
+def down(quarter, hot, spread, hot_spread, hidden, hhidden, w_down, part):
+    n, f, width = w_down.shape
+    tok, slots = spread.shape
+    rows = hidden.shape[1]
+    hrows = hhidden.shape[0]
+    half = tok // 2
+    scal = jnp.stack([quarter, hot]).astype(jnp.int32)
+
+    def whole(a):
+        return pl.BlockSpec(a.shape, lambda e, s: (0,) * a.ndim)
+
+    out = jax.ShapeDtypeStruct((half, part), BF16)
+    return pl.pallas_call(
+        down_kernel,
+        grid_spec=pltpu.PrefetchScalarGridSpec(
+            num_scalar_prefetch=1,
+            grid=(n,),
+            in_specs=[
+                whole(spread),
+                whole(hot_spread),
+                pl.BlockSpec((1, rows, f), lambda e, s: (e, 0, 0)),
+                whole(hhidden),
+                pl.BlockSpec((1, f, part), lambda e, s: (e, 0, s[0])),
+            ],
+            out_specs=(pl.BlockSpec(out.shape, lambda e, s: (0, 0)),) * 2,
+            scratch_shapes=[pltpu.VMEM((n * rows, part), BF16), pltpu.VMEM((hrows, part), BF16)],
+        ),
+        out_shape=(out, out),
+        compiler_params=pltpu.CompilerParams(vmem_limit_bytes=VMEM_LIMIT),
+        cost_estimate=pl.CostEstimate(
+            flops=2 * n * rows * part * f + 2 * n * rows * tok * part,
+            bytes_accessed=2 * n * part * f + 4 * tok * part,
+            transcendentals=0,
+        ),
+        name="down",
+    )(scal, spread, hot_spread, hidden, hhidden, w_down)
+
+
+def mover(n_dp, n_ex, step):
+    pairs = []
+    for d in range(n_dp):
+        for e in range(n_ex):
+            d2, z2, c2 = step(d, e // 2, e % 2)
+            pairs.append((d * n_ex + e, d2 * n_ex + z2 * 2 + c2))
+    return lambda x: lax.ppermute(x, AXES, pairs)
+
+
+def gather_local(n_dp, n_ex, tokens, routing, combine, w_gate, w_up, w_down):
+    lines = n_ex // 2
+    rows = tokens[0]
+    group_tok, width = rows.shape
+    top_k = routing.shape[2]
+    n = w_gate.shape[0]
+    part = width // n_dp
+    dp, me = lax.axis_index("dp"), lax.axis_index("expert")
+    along = [mover(n_dp, n_ex, lambda d, z, c, s=s: (d, (z + s) % lines, c)) for s in range(lines)]
+    across = [mover(n_dp, n_ex, lambda d, z, c, r=r: (d ^ r, z, c)) for r in range(n_dp)]
+    swap = mover(n_dp, n_ex, lambda d, z, c: (d, z, 1 - c))
+
+    info = jnp.concatenate([routing[0].astype(F32), combine[0]], axis=1).T
+    column = jnp.concatenate([info] + [along[s](info) for s in range(1, lines)], axis=1)
+    table = jnp.concatenate([column, swap(column)], axis=1)
+    tok = table.shape[1]
+
+    mine = [lax.dynamic_slice(rows, (0, (dp ^ r) * part), (group_tok, part)) for r in range(n_dp)]
+    far = [along[s](mine[0]) for s in range(1, lines)]
+    halves = []
+    for r in range(n_dp):
+        got = far if r == 0 else [across[r](piece) for piece in far]
+        halves.append(jnp.concatenate([mine[r]] + got, axis=0))
+    others = [swap(piece) for piece in halves]
+
+    cold_rows = -(-CAP * n_ex // 16) * 16
+    hot_rows = HOT_CAP * n_ex
+    picks = table[:top_k].astype(jnp.int32)
+    weights = table[top_k:]
+    here = picks[None] == (me * n + jnp.arange(n, dtype=jnp.int32))[:, None, None]
+    member = jnp.any(here, axis=1)
+    weight = jnp.sum(jnp.where(here, weights[None], 0.0), axis=1)
+    count = jnp.sum(member.astype(jnp.int32), axis=1)
+    busiest = count > CAP * n_ex
+    hot = jnp.where(jnp.any(busiest), jnp.argmax(busiest), -1).astype(jnp.int32)
+    upto = (jnp.arange(tok)[:, None] <= jnp.arange(tok)[None, :]).astype(BF16)
+    rank = jnp.dot(member.astype(BF16), upto, preferred_element_type=F32).astype(jnp.int32) - 1
+    place = jnp.where(member & ~busiest[:, None], rank, -1)
+    hot_place = jnp.max(jnp.where(member & busiest[:, None], rank, -1), axis=0)
+    hot_weight = jnp.sum(jnp.where(busiest[:, None], weight, 0.0), axis=0)
+    sit = place[:, None, :] == jnp.arange(cold_rows, dtype=jnp.int32)[None, :, None]
+    hot_sit = hot_place[None, :] == jnp.arange(hot_rows, dtype=jnp.int32)[:, None]
+    onehot = sit.astype(BF16).reshape(n * cold_rows, tok)
+    hot_onehot = hot_sit.astype(BF16)
+    scale = jnp.sum(jnp.where(sit, weight[:, None, :], 0.0), axis=2)[:, :, None]
+    hot_scale = jnp.sum(jnp.where(hot_sit, hot_weight[None, :], 0.0), axis=1)[:, None]
+    spread = onehot.T
+    hot_spread = hot_onehot.T
+
+    acc = None
+    for r in range(n_dp):
+        acc = gate_up(
+            dp ^ r, hot, onehot, hot_onehot, halves[r], others[r], w_gate, w_up, acc,
+            (scale, hot_scale) if r == n_dp - 1 else None,
+        )
+    hidden, hot_hidden = acc
+
+    total = None
+    for r in reversed(range(n_dp)):
+        own, other = down(dp ^ r, hot, spread, hot_spread, hidden, hot_hidden, w_down, part)
+        piece = (own.astype(F32) + swap(other).astype(F32)).astype(BF16)
+        if r:
+            piece = across[r](piece)
+        piece = piece.astype(F32)
+        total = piece if total is None else total + piece
+    total = total.astype(BF16)
+    out = total[:group_tok].astype(F32)
+    for s in range(1, lines):
+        out = out + along[lines - s](total[s * group_tok : (s + 1) * group_tok]).astype(F32)
+    return out.astype(BF16)[None]
+
+
 def solution(mesh):
     placed = (
         P("expert", None, None),
@@ -99,6 +345,9 @@
         P("expert", None, "dp"),
         P("expert", "dp", None),
     )
+    n_dp, n_ex = mesh.shape["dp"], mesh.shape["expert"]
+    short = n_ex <= 8 and n_ex % 2 == 0 and n_dp & (n_dp - 1) == 0
+    local = functools.partial(gather_local, n_dp, n_ex) if short else dispatch_local
     return jax.shard_map(
         local, mesh=mesh, in_specs=placed, out_specs=P("expert", None, "dp"), check_vma=False
     )

time: 686 us -> 229 us (0.33); the launches traced: 678 us -> 228 us
  waiting for transfers between devices: 321 us -> 57.9 us
  blocking collectives: 157 us -> 0 us
  Pallas kernels: 0 us -> 99.2 us
  matrix products: 79 us -> 0.23 us
  local copies, waits for them, and re-layouts: 75.5 us -> 11.2 us
  starting transfers between devices: 5.2 us -> 41.6 us
  between operations: 18.4 us -> 1.56 us
    all_to_all x1 -> x0, waiting for transfers between devices: 201 us -> none  [local(): lax.all_to_all(partial_value.astype(jnp.bfloat16), 'expert', split_axis=0...]
    all_to_all x1 -> x0, blocking collectives: 157 us -> none  [local(): lax.all_to_all(outgoing, 'expert', split_axis=0, concat_axis=0, tiled=True)]
    pallas_call x0 -> x8, Pallas kernels: none -> 99.2 us  [the longest x4 56.7 us: gate_up(): pl.pallas_call(functools.partial(gate_up_kernel, last, first), grid_spec=...]
    psum x1 -> x0, waiting for transfers between devices: 97.1 us -> none  [broadcast(): return lax.psum(block, axis)]
    dot_general x4 -> x1, matrix products: 79 us -> 0.23 us  [gather_local(): jnp.dot(member.astype(BF16), upto, preferred_element_type=F32)]
    ppermute x0 -> x30, waiting for transfers between devices: none -> 57.9 us  [mover(): return lambda x: lax.ppermute(x, AXES, pairs)]
    ppermute x0 -> x30, starting transfers between devices: none -> 41.6 us  [mover(): return lambda x: lax.ppermute(x, AXES, pairs)]
    reduce_scatter x2 -> x0, waiting for transfers between devices: 22.9 us -> none  [the longest x1 22.9 us: local(): lax.psum_scatter(hot_partial.astype(jnp.bfloat16), 'dp', scatter_dimensio...]
  transfers between devices with their start and end apart: 4 -> 30, of which waited for: 3 -> 10; matrix products, arithmetic and copies ran while one was open for 7% -> 10% of each run, Pallas kernels for 0% -> 33%
where the time goes in v1:
time: 229 us; the launch traced here: 228 us
  Pallas kernels  99.2 us (43%)
  waiting for transfers between devices  57.9 us (25%)
  starting transfers between devices  41.6 us (18%)
  other arithmetic  16.4 us (7%)
  local copies, waits for them, and re-layouts  11.2 us (5%)
    ppermute x30, waiting for transfers between devices, mover(): return lambda x: lax.ppermute(x, AXES, pairs)  57.9 us
    pallas_call x4, Pallas kernels, gate_up(): pl.pallas_call(functools.partial(gate_up_kernel, last, first), grid_spec=...  56.7 us
    pallas_call x4, Pallas kernels, down(): pl.pallas_call(down_kernel, grid_spec=pltpu.PrefetchScalarGridSpec(num_sc...  42.4 us
    ppermute x30, starting transfers between devices, mover(): return lambda x: lax.ppermute(x, AXES, pairs)  41.6 us
  transfers between devices with their start and end apart: 30, of which 10 were waited for; matrix products, arithmetic and copies ran while one was open for 10% of the time, Pallas kernels for 33%

profile of v1, /device:TPU:0, one launch (start us, length us, event | category | flops | bytes accessed | tf_op | source)
XLA Modules:
  0.0 228.1 jit_solution(6477621357365864283)
XLA Ops:
  1.4 3.0 %collective-permute-start = (f32[16,88]{1,0:T(8,128)S(1)}, f32[16,88]{1,0:T(8,128)S(1)}, u32[]{:S(2)}, u32[]{:S(2)}) collective-permute-start(f32[16,88]{1,0:T(8,128)S(1)} %maximum_bitcast_fusion), channel_id=1, source_target_pairs={{0,2},{1,3},{2,4},{3,5},{4,6},{5,7},{6,0},{7,1},{8,10},{9,11},{10,... | collective-permute-start | bytes 16904 | tf_op jit(solution)/shard_map/ppermute | solution.py:264
  4.4 2.6 %collective-permute-start.1 = (f32[16,88]{1,0:T(8,128)S(1)}, f32[16,88]{1,0:T(8,128)S(1)}, u32[]{:S(2)}, u32[]{:S(2)}) collective-permute-start(f32[16,88]{1,0:T(8,128)S(1)} %maximum_bitcast_fusion), channel_id=1, source_target_pairs={{0,4},{1,5},{2,6},{3,7},{4,0},{5,1},{6,2},{7,3},{8,12},{9,13},{10,... | collective-permute-start | bytes 16904 | tf_op jit(solution)/shard_map/ppermute | solution.py:264
  10.7 2.8 %collective-permute-start.8 = (bf16[88,1024]{1,0:T(8,128)(2,1)S(1)}, bf16[88,1024]{1,0:T(8,128)(2,1)}, u32[]{:S(2)}, u32[]{:S(2)}) collective-permute-start(bf16[88,1024]{1,0:T(8,128)(2,1)S(1)} %get-tuple-element.43), channel_id=1, source_target_pairs={{0,6},{1,7},{2,0},{3,1},{4,2},{5,3},{6,4},{7,5},{8,14},{9,15},{10,... | collective-permute-start | bytes 540680 | tf_op jit(solution)/shard_map/ppermute | solution.py:264
  16.7 1.8 eq.62
  18.5 2.5 %copy.20 = s32[896,704]{0,1:T(8,128)S(1)} copy(s32[896,704]{1,0:T(8,128)} %bitcast.25) | data formatting | bytes 5046272 | tf_op jit(solution)/shard_map/eq | solution.py:307
  32.8 1.6 collective-permute-start.11
  37.2 2.3 %collective-permute-done.16 = bf16[88,1024]{1,0:T(8,128)(2,1)S(1)} collective-permute-done((bf16[88,1024]{1,0:T(8,128)(2,1)S(1)}, bf16[88,1024]{1,0:T(8,128)(2,1)S(1)}, u32[]{:S(2)}, u32[]{:S(2)}) %collective-permute-start.16) | collective-permute-done | bytes 180256 | tf_op jit(solution)/shard_map/ppermute | solution.py:264
  42.7 2.4 %collective-permute-start.5 = (bf16[88,1024]{1,0:T(8,128)(2,1)}, bf16[88,1024]{1,0:T(8,128)(2,1)}, u32[]{:S(2)}, u32[]{:S(2)}) collective-permute-start(bf16[88,1024]{1,0:T(8,128)(2,1)} %collective-permute-done.4), channel_id=1, source_target_pairs={{0,24},{1,25},{2,26},{3,27},{4,28},{5,29},{6,30},{7,31},{8,16},{9,... | collective-permute-start | bytes 540680 | tf_op jit(solution)/shard_map/ppermute | solution.py:264
  46.0 2.0 copy.24.onehot
  55.1 2.9 %collective-permute-done.7 = bf16[88,1024]{1,0:T(8,128)(2,1)S(1)} collective-permute-done((bf16[88,1024]{1,0:T(8,128)(2,1)S(1)}, bf16[88,1024]{1,0:T(8,128)(2,1)S(1)}, u32[]{:S(2)}, u32[]{:S(2)}) %collective-permute-start.7) | collective-permute-done | bytes 180256 | tf_op jit(solution)/shard_map/ppermute | solution.py:264
  58.0 3.4 %collective-permute-done.9 = bf16[88,1024]{1,0:T(8,128)(2,1)S(1)} collective-permute-done((bf16[88,1024]{1,0:T(8,128)(2,1)}, bf16[88,1024]{1,0:T(8,128)(2,1)S(1)}, u32[]{:S(2)}, u32[]{:S(2)}) %collective-permute-start.9) | collective-permute-done | bytes 180256 | tf_op jit(solution)/shard_map/ppermute | solution.py:264
  62.5 13.5 %gate_up.4 = (f32[8,112,768]{2,1,0:T(8,128)}, f32[352,768]{1,0:T(8,128)}) custom-call(s32[2]{0:T(128)} %pad_add_fusion.3.scal, bf16[896,704]{1,0:T(8,128)(2,1)} %copy.24.onehot, bf16[352,704]{1,0:T(8,128)(2,1)} %fusion.3.hot_onehot, bf16[352,1024]{1,0:T(8,128)(2,1)} %copy-done.2, bf16[352,1024]{1,0:T(8,128)(2,1)} %collective-permute-done.19.xb, ...), custom_call_target="tpu_custom_call" | custom-call | flops 2701131776 | bytes 14024704 | tf_op jit(solution)/shard_map/gate_up/pallas_call | solution.py:171
  76.0 14.6 %gate_up.5 = (f32[8,112,768]{2,1,0:T(8,128)}, f32[352,768]{1,0:T(8,128)}) custom-call(s32[2]{0:T(128)} %pad_add_fusion.2.scal, bf16[896,704]{1,0:T(8,128)(2,1)} %copy.24.onehot, bf16[352,704]{1,0:T(8,128)(2,1)} %fusion.3.hot_onehot, bf16[352,1024]{1,0:T(8,128)(2,1)} %copy-done.3, bf16[352,1024]{1,0:T(8,128)(2,1)} %collective-permute-done.18.xb, ...), custom_call_target="tpu_custom_call" | custom-call | flops 2701131776 | bytes 14024704 | tf_op jit(solution)/shard_map/gate_up/pallas_call | solution.py:171
  91.4 14.8 %gate_up.6 = (f32[8,112,768]{2,1,0:T(8,128)}, f32[352,768]{1,0:T(8,128)}) custom-call(s32[2]{0:T(128)} %pad_add_fusion.1.scal, bf16[896,704]{1,0:T(8,128)(2,1)} %copy.24.onehot, bf16[352,704]{1,0:T(8,128)(2,1)} %fusion.3.hot_onehot, bf16[352,1024]{1,0:T(8,128)(2,1)} %copy-done.4, bf16[352,1024]{1,0:T(8,128)(2,1)} %copy-done.10, bf16[8,4096,384]{2,1,0:T(8,128)(2,1)} %wg.7, ...), custom_call_target="tpu_custom_call" | custom-call | flops 2701131776 | bytes 14024704 | tf_op jit(solution)/shard_map/gate_up/pallas_call | solution.py:171
  107.1 13.9 %gate_up.7 = (bf16[8,112,384]{2,1,0:T(8,128)(2,1)}, bf16[352,384]{1,0:T(8,128)(2,1)}) custom-call(s32[2]{0:T(128)} %pad_add_fusion.scal, bf16[896,704]{1,0:T(8,128)(2,1)} %copy.24.onehot, bf16[352,704]{1,0:T(8,128)(2,1)} %fusion.3.hot_onehot, bf16[352,1024]{1,0:T(8,128)(2,1)} %copy-done.1, bf16[352,1024]{1,0:T(8,128)(2,1)} %copy-done.5, ...), custom_call_target="tpu_custom_call" | custom-call | flops 2701131776 | bytes 14024704 | tf_op jit(solution)/shard_map/gate_up/pallas_call | solution.py:171
  120.9 10.5 %down.4 = (bf16[352,1024]{1,0:T(8,128)(2,1)}, bf16[352,1024]{1,0:T(8,128)(2,1)}) custom-call(s32[2]{0:T(128)} %pad_add_fusion.scal, bf16[704,896]{1,0:T(8,128)(2,1)} %fusion.12.spread, bf16[704,352]{1,0:T(8,128)(2,1)} %fusion.4.hot_spread, bf16[8,112,384]{2,1,0:T(8,128)(2,1)} %get-tuple-element.29.hidden, bf16[352,384]{1,0:T(8,128)(2,1)} %get-tuple-element.30.hhidden, ...), custom_call_target="tpu_custom_call" | custom-call | flops 1996488704 | bytes 9175040 | tf_op jit(solution)/shard_map/down/pallas_call | solution.py:232
  132.0 10.5 %down.5 = (bf16[352,1024]{1,0:T(8,128)(2,1)}, bf16[352,1024]{1,0:T(8,128)(2,1)}) custom-call(s32[2]{0:T(128)} %pad_add_fusion.1.scal, bf16[704,896]{1,0:T(8,128)(2,1)} %fusion.12.spread, bf16[704,352]{1,0:T(8,128)(2,1)} %fusion.4.hot_spread, bf16[8,112,384]{2,1,0:T(8,128)(2,1)} %get-tuple-element.29.hidden, bf16[352,384]{1,0:T(8,128)(2,1)} %get-tuple-element.30.hhidden, ...), custom_call_target="tpu_custom_call" | custom-call | flops 1996488704 | bytes 9175040 | tf_op jit(solution)/shard_map/down/pallas_call | solution.py:232
  142.6 10.8 %down.6 = (bf16[352,1024]{1,0:T(8,128)(2,1)}, bf16[352,1024]{1,0:T(8,128)(2,1)}) custom-call(s32[2]{0:T(128)} %pad_add_fusion.2.scal, bf16[704,896]{1,0:T(8,128)(2,1)} %fusion.12.spread, bf16[704,352]{1,0:T(8,128)(2,1)} %fusion.4.hot_spread, bf16[8,112,384]{2,1,0:T(8,128)(2,1)} %get-tuple-element.29.hidden, bf16[352,384]{1,0:T(8,128)(2,1)} %get-tuple-element.30.hhidden, ...), custom_call_target="tpu_custom_call" | custom-call | flops 1996488704 | bytes 9175040 | tf_op jit(solution)/shard_map/down/pallas_call | solution.py:232
  153.8 10.6 %down.7 = (bf16[352,1024]{1,0:T(8,128)(2,1)}, bf16[352,1024]{1,0:T(8,128)(2,1)}) custom-call(s32[2]{0:T(128)} %pad_add_fusion.3.scal, bf16[704,896]{1,0:T(8,128)(2,1)} %fusion.12.spread, bf16[704,352]{1,0:T(8,128)(2,1)} %fusion.4.hot_spread, bf16[8,112,384]{2,1,0:T(8,128)(2,1)} %get-tuple-element.29.hidden, bf16[352,384]{1,0:T(8,128)(2,1)} %get-tuple-element.30.hhidden, ...), custom_call_target="tpu_custom_call" | custom-call | flops 1996488704 | bytes 9175040 | tf_op jit(solution)/shard_map/down/pallas_call | solution.py:232
  169.1 15.7 %collective-permute-done.21 = bf16[352,1024]{1,0:T(8,128)(2,1)S(1)} collective-permute-done((bf16[352,1024]{1,0:T(8,128)(2,1)S(1)}, bf16[352,1024]{1,0:T(8,128)(2,1)S(1)}, u32[]{:S(2)}, u32[]{:S(2)}) %collective-permute-start.21) | collective-permute-done | bytes 720928 | tf_op jit(solution)/shard_map/ppermute | solution.py:264
  184.8 14.7 %collective-permute-done.23 = bf16[352,1024]{1,0:T(8,128)(2,1)S(1)} collective-permute-done((bf16[352,1024]{1,0:T(8,128)(2,1)S(1)}, bf16[352,1024]{1,0:T(8,128)(2,1)S(1)}, u32[]{:S(2)}, u32[]{:S(2)}) %collective-permute-start.23) | collective-permute-done | bytes 720928 | tf_op jit(solution)/shard_map/ppermute | solution.py:264
  201.6 9.9 %collective-permute-start.28 = (bf16[88,1024]{1,0:T(8,128)(2,1)S(1)}, bf16[88,1024]{1,0:T(8,128)(2,1)S(1)}, u32[]{:S(2)}, u32[]{:S(2)}) collective-permute-start(bf16[88,1024]{1,0:T(8,128)(2,1)S(1)} %get-tuple-element.41), channel_id=1, source_target_pairs={{0,4},{1,5},{2,6},{3,7},{4,0},{5,1},{6,2},{7,3},{8,12},{9,13},{10,... | collective-permute-start | bytes 540680 | tf_op jit(solution)/shard_map/ppermute | solution.py:264
  211.4 1.9 collective-permute-start.29
  213.4 13.9 %collective-permute-done.28 = bf16[88,1024]{1,0:T(8,128)(2,1)S(1)} collective-permute-done((bf16[88,1024]{1,0:T(8,128)(2,1)S(1)}, bf16[88,1024]{1,0:T(8,128)(2,1)S(1)}, u32[]{:S(2)}, u32[]{:S(2)}) %collective-permute-start.28) | collective-permute-done | bytes 180256 | tf_op jit(solution)/shard_map/ppermute | solution.py:264
  (107 shorter events, 43.9 us)
Async XLA Ops:
  1.4 9.3 %collective-permute-start = (f32[16,88]{1,0:T(8,128)S(1)}, f32[16,88]{1,0:T(8,128)S(1)}, u32[]{:S(2)}, u32[]{:S(2)}) collective-permute-start(f32[16,88]{1,0:T(8,128)S(1)} %maximum_bitcast_fusion), channel_id=1, source_target_pairs={{0,2},{1,3},{2,4},{3,5},{4,6},{5,7},{6,0},{7,1},{8,10},{9,11},{10,... | collective-permute-start | bytes 16904 | tf_op jit(solution)/shard_map/ppermute | solution.py:264
  9.6 18.5 %collective-permute-start.4 = (bf16[88,1024]{1,0:T(8,128)(2,1)S(1)}, bf16[88,1024]{1,0:T(8,128)(2,1)}, u32[]{:S(2)}, u32[]{:S(2)}) collective-permute-start(bf16[88,1024]{1,0:T(8,128)(2,1)S(1)} %get-tuple-element.43), channel_id=1, source_target_pairs={{0,2},{1,3},{2,4},{3,5},{4,6},{5,7},{6,0},{7,1},{8,10},{9,11},{10,... | collective-permute-start | bytes 540680 | tf_op jit(solution)/shard_map/ppermute | solution.py:264
  10.3 19.3 %collective-permute-start.6 = (bf16[88,1024]{1,0:T(8,128)(2,1)S(1)}, bf16[88,1024]{1,0:T(8,128)(2,1)S(1)}, u32[]{:S(2)}, u32[]{:S(2)}) collective-permute-start(bf16[88,1024]{1,0:T(8,128)(2,1)S(1)} %get-tuple-element.43), channel_id=1, source_target_pairs={{0,4},{1,5},{2,6},{3,7},{4,0},{5,1},{6,2},{7,3},{8,12},{9,13},{10,... | collective-permute-start | bytes 540680 | tf_op jit(solution)/shard_map/ppermute | solution.py:264
  10.7 19.5 %collective-permute-start.8 = (bf16[88,1024]{1,0:T(8,128)(2,1)S(1)}, bf16[88,1024]{1,0:T(8,128)(2,1)}, u32[]{:S(2)}, u32[]{:S(2)}) collective-permute-start(bf16[88,1024]{1,0:T(8,128)(2,1)S(1)} %get-tuple-element.43), channel_id=1, source_target_pairs={{0,6},{1,7},{2,0},{3,1},{4,2},{5,3},{6,4},{7,5},{8,14},{9,15},{10,... | collective-permute-start | bytes 540680 | tf_op jit(solution)/shard_map/ppermute | solution.py:264
  29.6 10.0 %collective-permute-start.16 = (bf16[88,1024]{1,0:T(8,128)(2,1)S(1)}, bf16[88,1024]{1,0:T(8,128)(2,1)S(1)}, u32[]{:S(2)}, u32[]{:S(2)}) collective-permute-start(bf16[88,1024]{1,0:T(8,128)(2,1)S(1)} %collective-permute-done.6), channel_id=1, source_target_pairs={{0,8},{1,9},{2,10},{3,11},{4,12},{5,13},{6,14},{7,15},{8,0},{9,1},... | collective-permute-start | bytes 540680 | tf_op jit(solution)/shard_map/ppermute | solution.py:264
  30.2 12.5 %collective-permute-start.17 = (bf16[88,1024]{1,0:T(8,128)(2,1)}, bf16[88,1024]{1,0:T(8,128)(2,1)S(1)}, u32[]{:S(2)}, u32[]{:S(2)}) collective-permute-start(bf16[88,1024]{1,0:T(8,128)(2,1)} %collective-permute-done.8), channel_id=1, source_target_pairs={{0,8},{1,9},{2,10},{3,11},{4,12},{5,13},{6,14},{7,15},{8,0},{9,1},... | collective-permute-start | bytes 540680 | tf_op jit(solution)/shard_map/ppermute | solution.py:264
  32.7 29.7 %collective-permute-start.19 = (bf16[352,1024]{1,0:T(8,128)(2,1)S(1)}, bf16[352,1024]{1,0:T(8,128)(2,1)}, u32[]{:S(2)}, u32[]{:S(2)}) collective-permute-start(bf16[352,1024]{1,0:T(8,128)(2,1)S(1)} %pad_maximum_fusion.3.xa), channel_id=1, source_target_pairs={{0,1},{1,0},{2,3},{3,2},{4,5},{5,4},{6,7},{7,6},{8,9},{9,8},{10,11... | collective-permute-start | bytes 2162696 | tf_op jit(solution)/shard_map/ppermute | solution.py:264
  32.8 12.4 %collective-permute-start.11 = (bf16[88,1024]{1,0:T(8,128)(2,1)}, bf16[88,1024]{1,0:T(8,128)(2,1)}, u32[]{:S(2)}, u32[]{:S(2)}) collective-permute-start(bf16[88,1024]{1,0:T(8,128)(2,1)} %collective-permute-done.4), channel_id=1, source_target_pairs={{0,16},{1,17},{2,18},{3,19},{4,20},{5,21},{6,22},{7,23},{8,24},{9,... | collective-permute-start | bytes 540680 | tf_op jit(solution)/shard_map/ppermute | solution.py:264
  35.7 14.0 %collective-permute-start.12 = (bf16[88,1024]{1,0:T(8,128)(2,1)S(1)}, bf16[88,1024]{1,0:T(8,128)(2,1)}, u32[]{:S(2)}, u32[]{:S(2)}) collective-permute-start(bf16[88,1024]{1,0:T(8,128)(2,1)S(1)} %collective-permute-done.6), channel_id=1, source_target_pairs={{0,16},{1,17},{2,18},{3,19},{4,20},{5,21},{6,22},{7,23},{8,24},{9,... | collective-permute-start | bytes 540680 | tf_op jit(solution)/shard_map/ppermute | solution.py:264
  39.6 12.1 %collective-permute-start.13 = (bf16[88,1024]{1,0:T(8,128)(2,1)}, bf16[88,1024]{1,0:T(8,128)(2,1)}, u32[]{:S(2)}, u32[]{:S(2)}) collective-permute-start(bf16[88,1024]{1,0:T(8,128)(2,1)} %collective-permute-done.8), channel_id=1, source_target_pairs={{0,16},{1,17},{2,18},{3,19},{4,20},{5,21},{6,22},{7,23},{8,24},{9,... | collective-permute-start | bytes 540680 | tf_op jit(solution)/shard_map/ppermute | solution.py:264
  42.7 11.6 %collective-permute-start.5 = (bf16[88,1024]{1,0:T(8,128)(2,1)}, bf16[88,1024]{1,0:T(8,128)(2,1)}, u32[]{:S(2)}, u32[]{:S(2)}) collective-permute-start(bf16[88,1024]{1,0:T(8,128)(2,1)} %collective-permute-done.4), channel_id=1, source_target_pairs={{0,24},{1,25},{2,26},{3,27},{4,28},{5,29},{6,30},{7,31},{8,16},{9,... | collective-permute-start | bytes 540680 | tf_op jit(solution)/shard_map/ppermute | solution.py:264
  45.2 30.8 %collective-permute-start.18 = (bf16[352,1024]{1,0:T(8,128)(2,1)S(1)}, bf16[352,1024]{1,0:T(8,128)(2,1)}, u32[]{:S(2)}, u32[]{:S(2)}) collective-permute-start(bf16[352,1024]{1,0:T(8,128)(2,1)S(1)} %pad_maximum_fusion.2.xa), channel_id=1, source_target_pairs={{0,1},{1,0},{2,3},{3,2},{4,5},{5,4},{6,7},{7,6},{8,9},{9,8},{10,11... | collective-permute-start | bytes 2162696 | tf_op jit(solution)/shard_map/ppermute | solution.py:264
  51.7 9.7 %collective-permute-start.9 = (bf16[88,1024]{1,0:T(8,128)(2,1)}, bf16[88,1024]{1,0:T(8,128)(2,1)S(1)}, u32[]{:S(2)}, u32[]{:S(2)}) collective-permute-start(bf16[88,1024]{1,0:T(8,128)(2,1)} %collective-permute-done.8), channel_id=1, source_target_pairs={{0,24},{1,25},{2,26},{3,27},{4,28},{5,29},{6,30},{7,31},{8,16},{9,... | collective-permute-start | bytes 540680 | tf_op jit(solution)/shard_map/ppermute | solution.py:264
  54.3 36.3 %collective-permute-start.14 = (bf16[352,1024]{1,0:T(8,128)(2,1)S(1)}, bf16[352,1024]{1,0:T(8,128)(2,1)S(1)}, u32[]{:S(2)}, u32[]{:S(2)}) collective-permute-start(bf16[352,1024]{1,0:T(8,128)(2,1)S(1)} %pad_maximum_fusion.1.xa), channel_id=1, source_target_pairs={{0,1},{1,0},{2,3},{3,2},{4,5},{5,4},{6,7},{7,6},{8,9},{9,8},{10,11... | collective-permute-start | bytes 2162696 | tf_op jit(solution)/shard_map/ppermute | solution.py:264
  62.4 43.8 %collective-permute-start.10 = (bf16[352,1024]{1,0:T(8,128)(2,1)S(1)}, bf16[352,1024]{1,0:T(8,128)(2,1)S(1)}, u32[]{:S(2)}, u32[]{:S(2)}) collective-permute-start(bf16[352,1024]{1,0:T(8,128)(2,1)S(1)} %pad_maximum_fusion.xa), channel_id=1, source_target_pairs={{0,1},{1,0},{2,3},{3,2},{4,5},{5,4},{6,7},{7,6},{8,9},{9,8},{10,11... | collective-permute-start | bytes 2162696 | tf_op jit(solution)/shard_map/ppermute | solution.py:264
  131.5 33.1 %collective-permute-start.20 = (bf16[352,1024]{1,0:T(8,128)(2,1)}, bf16[352,1024]{1,0:T(8,128)(2,1)S(1)}, u32[]{:S(2)}, u32[]{:S(2)}) collective-permute-start(bf16[352,1024]{1,0:T(8,128)(2,1)} %get-tuple-element.32), channel_id=1, source_target_pairs={{0,1},{1,0},{2,3},{3,2},{4,5},{5,4},{6,7},{7,6},{8,9},{9,8},{10,11... | collective-permute-start | bytes 2162696 | tf_op jit(solution)/shard_map/ppermute | solution.py:264
  142.5 22.9 %collective-permute-start.22 = (bf16[352,1024]{1,0:T(8,128)(2,1)}, bf16[352,1024]{1,0:T(8,128)(2,1)S(1)}, u32[]{:S(2)}, u32[]{:S(2)}) collective-permute-start(bf16[352,1024]{1,0:T(8,128)(2,1)} %get-tuple-element.34), channel_id=1, source_target_pairs={{0,1},{1,0},{2,3},{3,2},{4,5},{5,4},{6,7},{7,6},{8,9},{9,8},{10,11... | collective-permute-start | bytes 2162696 | tf_op jit(solution)/shard_map/ppermute | solution.py:264
  153.3 13.9 %collective-permute-start.24 = (bf16[352,1024]{1,0:T(8,128)(2,1)}, bf16[352,1024]{1,0:T(8,128)(2,1)S(1)}, u32[]{:S(2)}, u32[]{:S(2)}) collective-permute-start(bf16[352,1024]{1,0:T(8,128)(2,1)} %get-tuple-element.36), channel_id=1, source_target_pairs={{0,1},{1,0},{2,3},{3,2},{4,5},{5,4},{6,7},{7,6},{8,9},{9,8},{10,11... | collective-permute-start | bytes 2162696 | tf_op jit(solution)/shard_map/ppermute | solution.py:264
  164.8 20.0 %collective-permute-start.21 = (bf16[352,1024]{1,0:T(8,128)(2,1)S(1)}, bf16[352,1024]{1,0:T(8,128)(2,1)S(1)}, u32[]{:S(2)}, u32[]{:S(2)}) collective-permute-start(bf16[352,1024]{1,0:T(8,128)(2,1)S(1)} %add_convert_fusion.4), channel_id=1, source_target_pairs={{0,24},{1,25},{2,26},{3,27},{4,28},{5,29},{6,30},{7,31},{8,16},{9,... | collective-permute-start | bytes 2162696 | tf_op jit(solution)/shard_map/ppermute | solution.py:264
  165.8 33.7 %collective-permute-start.23 = (bf16[352,1024]{1,0:T(8,128)(2,1)S(1)}, bf16[352,1024]{1,0:T(8,128)(2,1)S(1)}, u32[]{:S(2)}, u32[]{:S(2)}) collective-permute-start(bf16[352,1024]{1,0:T(8,128)(2,1)S(1)} %add_convert_fusion.3), channel_id=1, source_target_pairs={{0,16},{1,17},{2,18},{3,19},{4,20},{5,21},{6,22},{7,23},{8,24},{9,... | collective-permute-start | bytes 2162696 | tf_op jit(solution)/shard_map/ppermute | solution.py:264
  167.5 32.0 %collective-permute-start.25 = (bf16[352,1024]{1,0:T(8,128)(2,1)S(1)}, bf16[352,1024]{1,0:T(8,128)(2,1)S(1)}, u32[]{:S(2)}, u32[]{:S(2)}) collective-permute-start(bf16[352,1024]{1,0:T(8,128)(2,1)S(1)} %add_convert_fusion.2), channel_id=1, source_target_pairs={{0,8},{1,9},{2,10},{3,11},{4,12},{5,13},{6,14},{7,15},{8,0},{9,1},... | collective-permute-start | bytes 2162696 | tf_op jit(solution)/shard_map/ppermute | solution.py:264
  200.3 13.1 %collective-permute-start.27 = (bf16[88,1024]{1,0:T(8,128)(2,1)S(1)}, bf16[88,1024]{1,0:T(8,128)(2,1)S(1)}, u32[]{:S(2)}, u32[]{:S(2)}) collective-permute-start(bf16[88,1024]{1,0:T(8,128)(2,1)S(1)} %get-tuple-element.39), channel_id=1, source_target_pairs={{0,6},{1,7},{2,0},{3,1},{4,2},{5,3},{6,4},{7,5},{8,14},{9,15},{10,... | collective-permute-start | bytes 540680 | tf_op jit(solution)/shard_map/ppermute | solution.py:264
  201.6 25.8 %collective-permute-start.28 = (bf16[88,1024]{1,0:T(8,128)(2,1)S(1)}, bf16[88,1024]{1,0:T(8,128)(2,1)S(1)}, u32[]{:S(2)}, u32[]{:S(2)}) collective-permute-start(bf16[88,1024]{1,0:T(8,128)(2,1)S(1)} %get-tuple-element.41), channel_id=1, source_target_pairs={{0,4},{1,5},{2,6},{3,7},{4,0},{5,1},{6,2},{7,3},{8,12},{9,13},{10,... | collective-permute-start | bytes 540680 | tf_op jit(solution)/shard_map/ppermute | solution.py:264
  211.4 15.9 %collective-permute-start.29 = (bf16[88,1024]{1,0:T(8,128)(2,1)S(1)}, bf16[88,1024]{1,0:T(8,128)(2,1)S(1)}, u32[]{:S(2)}, u32[]{:S(2)}) collective-permute-start(bf16[88,1024]{1,0:T(8,128)(2,1)S(1)} %get-tuple-element.40), channel_id=1, source_target_pairs={{0,2},{1,3},{2,4},{3,5},{4,6},{5,7},{6,0},{7,1},{8,10},{9,11},{10,... | collective-permute-start | bytes 540680 | tf_op jit(solution)/shard_map/ppermute | solution.py:264
  (17 other events, 160.0 us)

commit v2 on v0

--- a/solution.py
+++ b/solution.py
@@ -1,10 +1,19 @@
+import functools
+
 import jax
 import jax.numpy as jnp
 from jax import lax
+from jax.experimental import pallas as pl
+from jax.experimental.pallas import tpu as pltpu
 from jax.sharding import PartitionSpec as P
 
 CAP = 13
 HOT_CAP = 44
+AXES = ("dp", "expert")
+BF16 = jnp.bfloat16
+F32 = jnp.float32
+VMEM_LIMIT = 60 * 1024 * 1024
+COST = 0
 
 
 def broadcast(block, axis, holder):
@@ -19,7 +28,7 @@
     return jnp.dot(hidden, down_mat, preferred_element_type=jnp.float32)
 
 
-def local(tokens, routing, combine, w_gate, w_up, w_down):
+def dispatch_local(tokens, routing, combine, w_gate, w_up, w_down):
     group_rows = tokens[0]
     chosen = routing[0]
     mixing = combine[0]
@@ -90,6 +99,446 @@
     return combined.astype(jnp.bfloat16)[None]
 
 
+def scalars():
+    return pl.BlockSpec(memory_space=pltpu.SMEM)
+
+
+def outside():
+    return pl.BlockSpec(memory_space=pltpu.HBM)
+
+
+def inside():
+    return pl.BlockSpec(memory_space=pltpu.VMEM)
+
+
+def staged_kernel(body, n_scalars, n_in, n_out, *refs):
+    given, rest = refs[:n_scalars], refs[n_scalars:]
+    far_in, far_out, rest = rest[:n_in], rest[n_in : n_in + n_out], rest[n_in + n_out :]
+    near_in, near_out, sem, rest = rest[-n_in - n_out - 1 : -n_out - 1], rest[-n_out - 1 : -1], rest[-1], rest[: -n_in - n_out - 1]
+    loads = [pltpu.make_async_copy(s, d, sem.at[i]) for i, (s, d) in enumerate(zip(far_in, near_in))]
+    for copy in loads:
+        copy.start()
+    for copy in loads:
+        copy.wait()
+    body(*given, *near_in, *near_out, *rest)
+    stores = [pltpu.make_async_copy(s, d, sem.at[n_in + i]) for i, (s, d) in enumerate(zip(near_out, far_out))]
+    for copy in stores:
+        copy.start()
+    for copy in stores:
+        copy.wait()
+
+
+def staged(body, given, inputs, outs, extra_outs=(), scratch=(), cost=1_000_000, name=None):
+    near = [pltpu.VMEM(a.shape, a.dtype) for a in list(inputs) + list(outs)]
+    return pl.pallas_call(
+        functools.partial(staged_kernel, body, len(given), len(inputs), len(outs)),
+        in_specs=[scalars()] * len(given) + [outside()] * len(inputs),
+        out_specs=(outside(),) * len(outs) + (scalars(),) * len(extra_outs),
+        out_shape=tuple(outs) + tuple(extra_outs),
+        scratch_shapes=list(scratch) + near + [pltpu.SemaphoreType.DMA((len(near),))],
+        compiler_params=pltpu.CompilerParams(vmem_limit_bytes=VMEM_LIMIT),
+        cost_estimate=pl.CostEstimate(flops=0, bytes_accessed=cost, transcendentals=0),
+        name=name,
+    )(*given, *inputs)
+
+
+def pack_kernel(first, *rest):
+    pieces, (near, tail, table) = rest[:-3], rest[-3:]
+    group_tok = first.shape[0]
+    width = near.shape[1]
+    table[len(pieces) * group_tok :, :] = first[:, width:]
+    tail[...] = pieces[-1][:, :width]
+    for i, piece in enumerate(pieces):
+        near[i * group_tok : (i + 1) * group_tok, :] = piece[:, :width]
+        table[i * group_tok : (i + 1) * group_tok, :] = piece[:, width:]
+
+
+def pack(first, pieces, width):
+    group_tok, lanes = first.shape
+    outs = (
+        jax.ShapeDtypeStruct((len(pieces) * group_tok, width), BF16),
+        jax.ShapeDtypeStruct((group_tok, width), BF16),
+        jax.ShapeDtypeStruct(((1 + len(pieces)) * group_tok, lanes - width), BF16),
+    )
+    return staged(pack_kernel, [], [first, *pieces], outs, name="pack")
+
+
+def places_kernel(top_k, cap, base, own, other, onehot, hot_onehot, spread, hot_spread, scale, hscale, hot_out, stage):
+    half = own.shape[0]
+    tok = 2 * half
+    n, rows = scale.shape[0], scale.shape[1]
+    hrows = hot_onehot.shape[0]
+    stage[0:half, :] = own[...].astype(F32)
+    stage[half:tok, :] = other[...].astype(F32)
+    table = stage[...].T
+    picks = table[0:top_k].astype(jnp.int32) - base[0]
+    weights = table[top_k : 2 * top_k] + table[2 * top_k : 3 * top_k] + table[3 * top_k : 4 * top_k]
+    here = [picks == e for e in range(n)]
+    member = jnp.concatenate([jnp.max(h.astype(F32), axis=0, keepdims=True) for h in here], axis=0)
+    weight = jnp.concatenate([jnp.sum(jnp.where(h, weights, 0.0), axis=0, keepdims=True) for h in here], axis=0)
+    busiest = jnp.sum(member, axis=1, keepdims=True) > cap
+    upto = lax.broadcasted_iota(jnp.int32, (tok, tok), 0) <= lax.broadcasted_iota(jnp.int32, (tok, tok), 1)
+    rank = jnp.dot(member.astype(BF16), upto.astype(F32).astype(BF16), preferred_element_type=F32) - 1.0
+    place = jnp.where((member > 0.0) & (rank < rows), rank, -1.0)
+    hot_place = jnp.max(jnp.where((member > 0.0) & busiest, rank - rows, -1.0), axis=0, keepdims=True)
+    hot_weight = jnp.sum(jnp.where(busiest, weight, 0.0), axis=0, keepdims=True)
+    number = lax.broadcasted_iota(jnp.int32, (n, 1), 0).astype(F32)
+    hot_out[0] = jnp.max(jnp.where(busiest, number, -1.0)).astype(jnp.int32)
+    slot = lax.broadcasted_iota(jnp.int32, (rows, tok), 0).astype(F32)
+    for e in range(n):
+        sit = slot == place[e : e + 1]
+        onehot[e * rows : (e + 1) * rows, :] = sit.astype(F32).astype(BF16)
+        scale[e] = jnp.sum(jnp.where(sit, weight[e : e + 1], 0.0), axis=1, keepdims=True)
+    slot = lax.broadcasted_iota(jnp.int32, (hrows, tok), 0).astype(F32)
+    sit = slot == hot_place
+    hot_onehot[...] = sit.astype(F32).astype(BF16)
+    hscale[...] = jnp.sum(jnp.where(sit, hot_weight, 0.0), axis=1, keepdims=True)
+    spread[...] = onehot[...].T
+    hot_spread[...] = hot_onehot[...].T
+
+
+def places(base, own, other, n, groups, top_k):
+    tok = 2 * own.shape[0]
+    rows = -(-CAP * groups // 16) * 16
+    hrows = -(-(HOT_CAP * groups - rows) // 16) * 16
+    outs = (
+        jax.ShapeDtypeStruct((n * rows, tok), BF16),
+        jax.ShapeDtypeStruct((hrows, tok), BF16),
+        jax.ShapeDtypeStruct((tok, n * rows), BF16),
+        jax.ShapeDtypeStruct((tok, hrows), BF16),
+        jax.ShapeDtypeStruct((n, rows, 1), F32),
+        jax.ShapeDtypeStruct((hrows, 1), F32),
+    )
+    return staged(
+        functools.partial(places_kernel, top_k, CAP * groups), [base], [own, other], outs,
+        [jax.ShapeDtypeStruct((1,), jnp.int32)], [pltpu.VMEM((tok, own.shape[1]), F32)], 15_000_000, "places",
+    )
+
+
+def gate_up_kernel(counts, first, last, depth, quarter, busy, wg, wu, mine, theirs, *rest):
+    nq = len(counts)
+    rest = list(rest)
+
+    def take(count):
+        taken, rest[:count] = rest[:count], []
+        return taken
+
+    far = [take(2 * count) for count in counts]
+    loaded = take(2 + (0 if first else 2) + (2 if last else 0))
+    out, hout = take(2)
+    near_v = [take(2 * count) for count in counts]
+    loaded_v = take(len(loaded))
+    onehot, hot_onehot = loaded_v[:2]
+    prev, hprev = (None, None) if first else loaded_v[2:4]
+    scale, hscale = loaded_v[-2:] if last else (None, None)
+    total, htotal = (out, hout) if last else take(2)
+    own, x, xg, xh, held, sem, load_sem, far_sem, own_sem, out_sem = rest
+    n, _, f = wg.shape
+    rows = xg.shape[1]
+    group_tok, part = own.shape[2:]
+    half = x.shape[0] // 2
+    hot = busy[0]
+
+    def start_of(i):
+        return pl.multiple_of(quarter[i] * part, part)
+
+    def copies(e, slot):
+        return [
+            pltpu.make_async_copy(
+                w.at[e, pl.ds(start_of(i), part), :],
+                held.at[slot, m, pl.ds(i * part, part), :],
+                sem.at[slot, m, i],
+            )
+            for m, w in enumerate((wg, wu))
+            for i in range(nq)
+        ]
+
+    loads = [pltpu.make_async_copy(s, d, load_sem.at[k]) for k, (s, d) in enumerate(zip(loaded, loaded_v))]
+    pieces = []
+    for i in range(nq):
+        group = [
+            pltpu.make_async_copy(w.at[:, pl.ds(start_of(i), part)], own.at[i, k], own_sem.at[i, k])
+            for k, w in enumerate((mine, theirs))
+        ]
+        group += [pltpu.make_async_copy(s, d, far_sem.at[i, k]) for k, (s, d) in enumerate(zip(far[i], near_v[i]))]
+        pieces.append(group)
+
+    def start(copies):
+        for copy in copies:
+            copy.start()
+
+    start(loads[:2] + pieces[0])
+    ahead = [copies(e, e) for e in range(min(depth, n))]
+    ahead = [sum(pieces[1:], [])] + ahead[:1] + [loads[2:]] + ahead[1:]
+    for i in range(nq):
+        lanes = slice(i * part, (i + 1) * part)
+        for copy in (loads[:2] if i == 0 else []) + pieces[i]:
+            copy.wait()
+        for _ in range(2 if i < nq - 1 else len(ahead)):
+            start(ahead.pop(0))
+        for k, values in enumerate((near_v[i][: counts[i]], near_v[i][counts[i] :])):
+            at = k * half
+            for value in values + [own.at[i, k]]:
+                x[at : at + value.shape[0]] = value[...]
+                at += value.shape[0]
+        picked = jnp.dot(onehot[...], x[...], preferred_element_type=F32).astype(BF16)
+        xg[:, :, lanes] = picked.reshape(n, rows, part)
+
+        @pl.when(hot >= 0)
+        def _(lanes=lanes):
+            xh[:, lanes] = jnp.dot(hot_onehot[...], x[...], preferred_element_type=F32).astype(BF16)
+
+    for copy in loads[2:]:
+        copy.wait()
+
+    def work(rows_in, slot, at, base, dst, scale_col):
+        low, high = at + (slice(None), slice(0, f)), at + (slice(None), slice(f, 2 * f))
+        g = jnp.dot(rows_in, held[slot, 0], preferred_element_type=F32)
+        u = jnp.dot(rows_in, held[slot, 1], preferred_element_type=F32)
+        if base is not None:
+            g = g + base[low]
+            u = u + base[high]
+        if last:
+            dst[at] = (g / (1.0 + jnp.exp(-g)) * u * scale_col).astype(BF16)
+        else:
+            dst[low] = g
+            dst[high] = u
+
+    def store(e):
+        return pltpu.make_async_copy(total.at[e], out.at[e], out_sem.at[e])
+
+    @pl.loop(0, n)
+    def _(e):
+        slot = lax.rem(e, depth)
+        for copy in copies(e, slot):
+            copy.wait()
+
+        work(xg[e], slot, (e,), prev, total, scale[e] if last else None)
+
+        @pl.when(e == hot)
+        def _():
+            work(xh[...], slot, (), hprev, htotal, hscale[...] if last else None)
+
+        @pl.when(e + depth < n)
+        def _():
+            for copy in copies(e + depth, slot):
+                copy.start()
+
+        if not last:
+            store(e).start()
+
+    if not last:
+        tail = pltpu.make_async_copy(htotal, hout, out_sem.at[n])
+        tail.start()
+        for e in range(n):
+            store(e).wait()
+        tail.wait()
+
+
+def gate_up(quarters, hot, onehot, hot_onehot, mine, theirs, got, w_gate, w_up, acc, scales):
+    n, width, f = w_gate.shape
+    tok = onehot.shape[1]
+    part = got[0][0].shape[1]
+    rows = onehot.shape[0] // n
+    hrows = hot_onehot.shape[0]
+    nq = len(got)
+    first, last = acc is None, scales is not None
+    depth = min(n, 4)
+    loaded = [onehot, hot_onehot] + ([] if first else list(acc)) + list(scales or ())
+    far = [piece for pieces in got for piece in pieces]
+    operands = [jnp.stack(quarters).astype(jnp.int32), hot, w_gate, w_up, mine, theirs] + far + loaded
+    specs = [scalars()] * 2 + [outside()] * (len(operands) - 2)
+    if last:
+        outs = (jax.ShapeDtypeStruct((n, rows, f), BF16), jax.ShapeDtypeStruct((hrows, f), BF16))
+    else:
+        outs = (jax.ShapeDtypeStruct((n, rows, 2 * f), F32), jax.ShapeDtypeStruct((hrows, 2 * f), F32))
+    scratch = [] if last else [pltpu.VMEM(o.shape, o.dtype) for o in outs]
+    return pl.pallas_call(
+        functools.partial(gate_up_kernel, tuple(len(p) // 2 for p in got), first, last, depth),
+        in_specs=specs,
+        out_specs=(inside(), inside()) if last else (outside(), outside()),
+        out_shape=outs,
+        scratch_shapes=[pltpu.VMEM(a.shape, a.dtype) for a in far + loaded]
+        + scratch
+        + [
+            pltpu.VMEM((nq, 2, mine.shape[0], part), BF16),
+            pltpu.VMEM((tok, part), BF16),
+            pltpu.VMEM((n, rows, nq * part), BF16),
+            pltpu.VMEM((hrows, nq * part), BF16),
+            pltpu.VMEM((depth, 2, nq * part, f), BF16),
+            pltpu.SemaphoreType.DMA((depth, 2, nq)),
+            pltpu.SemaphoreType.DMA((len(loaded),)),
+            pltpu.SemaphoreType.DMA((nq, max(len(p) for p in got))),
+            pltpu.SemaphoreType.DMA((nq, 2)),
+            pltpu.SemaphoreType.DMA((n + 1,)),
+        ],
+        compiler_params=pltpu.CompilerParams(vmem_limit_bytes=VMEM_LIMIT),
+        cost_estimate=pl.CostEstimate(
+            flops=0, bytes_accessed=COST * nq * n * part * f * 4, transcendentals=0
+        ),
+        name="gate_up",
+    )(*operands)
+
+
+def down_kernel(nq, quarter, busy, spread_far, hot_far, hidden, hhidden, wd, out_a, out_b, *scratch):
+    spread, hot_spread, y, yh, held, sem, load_sem = scratch
+    n, rows, _ = hidden.shape
+    half = out_a.shape[0]
+    part = y.shape[1]
+    hot = busy[0]
+
+    def copy(i, e):
+        column = pl.ds(pl.multiple_of(quarter[i] * part, part), part)
+        return pltpu.make_async_copy(wd.at[e, :, column], held.at[i, e], sem.at[i, e])
+
+    pairs = (spread_far, spread), (hot_far, hot_spread)
+    loads = [pltpu.make_async_copy(s, d, load_sem.at[k]) for k, (s, d) in enumerate(pairs)]
+    steps = [(i, e) for i in range(nq) for e in range(n)]
+    window = 6
+    for step in steps[:window]:
+        copy(*step).start()
+
+    for i in range(nq):
+        lanes = slice(i * part, (i + 1) * part)
+        for e in range(n):
+            copy(i, e).wait()
+            for step in steps[i * n + e + window : i * n + e + window + 1]:
+                copy(*step).start()
+            if i == 0 and e < 2:
+                loads[e].start()
+            y[e * rows : (e + 1) * rows, :] = jnp.dot(hidden[e], held[i, e], preferred_element_type=F32).astype(BF16)
+
+        @pl.when(hot >= 0)
+        def _():
+            yh[...] = jnp.dot(hhidden[...], held[i, hot], preferred_element_type=F32).astype(BF16)
+
+        if i == 0:
+            for load in loads:
+                load.wait()
+
+        @pl.when(hot < 0)
+        def _():
+            value = jnp.dot(spread[...], y[...], preferred_element_type=F32).astype(BF16)
+            out_a[:, lanes] = value[:half]
+            out_b[:, lanes] = value[half:]
+
+        @pl.when(hot >= 0)
+        def _():
+            value = jnp.dot(spread[...], y[...], preferred_element_type=F32)
+            value = value + jnp.dot(hot_spread[...], yh[...], preferred_element_type=F32)
+            value = value.astype(BF16)
+            out_a[:, lanes] = value[:half]
+            out_b[:, lanes] = value[half:]
+
+
+def down(quarters, hot, spread, hot_spread, hidden, hhidden, w_down, part):
+    n, f, width = w_down.shape
+    tok, slots = spread.shape
+    rows = hidden.shape[1]
+    hrows = hhidden.shape[0]
+    nq = len(quarters)
+    out = jax.ShapeDtypeStruct((tok // 2, nq * part), BF16)
+    return pl.pallas_call(
+        functools.partial(down_kernel, nq),
+        in_specs=[scalars()] * 2 + [outside()] * 2 + [inside()] * 2 + [outside()],
+        out_specs=(inside(), inside()),
+        out_shape=(out, out),
+        scratch_shapes=[
+            pltpu.VMEM(spread.shape, BF16),
+            pltpu.VMEM(hot_spread.shape, BF16),
+            pltpu.VMEM((n * rows, part), BF16),
+            pltpu.VMEM((hrows, part), BF16),
+            pltpu.VMEM((nq, n, f, part), BF16),
+            pltpu.SemaphoreType.DMA((nq, n)),
+            pltpu.SemaphoreType.DMA((2,)),
+        ],
+        compiler_params=pltpu.CompilerParams(vmem_limit_bytes=46 * 1024 * 1024),
+        cost_estimate=pl.CostEstimate(
+            flops=0, bytes_accessed=COST * 2 * nq * n * part * f * 2, transcendentals=0
+        ),
+        name="down",
+    )(jnp.stack(quarters).astype(jnp.int32), hot, spread, hot_spread, hidden, hhidden, w_down)
+
+
+def mover(n_dp, n_ex, step):
+    pairs = []
+    for d in range(n_dp):
+        for e in range(n_ex):
+            d2, z2, c2 = step(d, e // 2, e % 2)
+            pairs.append((d * n_ex + e, d2 * n_ex + z2 * 2 + c2))
+    return lambda x: lax.ppermute(x, AXES, pairs)
+
+
+def after(*values):
+    return lax.optimization_barrier(values)
+
+
+def gather_local(n_dp, n_ex, tokens, routing, combine, w_gate, w_up, w_down):
+    lines = n_ex // 2
+    rows = tokens[0]
+    group_tok, width = rows.shape
+    top_k = routing.shape[2]
+    n = w_gate.shape[0]
+    part = width // n_dp
+    cut = part // 2
+    dp, me = lax.axis_index("dp"), lax.axis_index("expert")
+    along = [mover(n_dp, n_ex, lambda d, z, c, s=s: (d, (z + s) % lines, c)) for s in range(lines)]
+    across = [mover(n_dp, n_ex, lambda d, z, c, r=r: (d ^ r, z, c)) for r in range(n_dp)]
+    swap = mover(n_dp, n_ex, lambda d, z, c: (d, z, 1 - c))
+    order = [1, 3, 2]
+
+    mine = [lax.dynamic_slice(rows, (0, (dp ^ r) * part), (group_tok, part)) for r in (0, 3)]
+    left, info = combine[0], [routing[0].astype(BF16)]
+    for _ in range(3):
+        term = lax.reduce_precision(left, 8, 7)
+        info.append(term.astype(BF16))
+        left = left - term
+    blank = jnp.zeros((group_tok, -4 * top_k % 128), BF16)
+    first = jnp.concatenate([mine[0]] + info + [blank], axis=1)
+    theirs = swap(rows)
+    got = after(theirs, *[along[s](first) for s in order])
+    theirs, got = got[0], got[1:]
+    corner = after(mine[1], *got)[0]
+    near, tail, table = pack(first, got, part)
+    corner = [along[s](corner) for s in order[:2]] + [across[3](tail)]
+    by_x, by_y = across[1](near), across[2](near)
+    table_other, near_other = swap(table), swap(near)
+    onehot, hot_onehot, spread, hot_spread, scale, hot_scale, hot = places(
+        (me * n).astype(jnp.int32)[None], table, table_other, n, n_ex, top_k
+    )
+    acc = gate_up([dp], hot, onehot, hot_onehot, rows, theirs, [[near, near_other]], w_gate, w_up, None, None)
+    acc, by_x, by_y, corner = after(acc, by_x, by_y, corner)
+    got = [list(pieces) + [swap(piece) for piece in pieces] for pieces in ((by_x,), (by_y,), corner)]
+    hidden, hot_hidden = gate_up(
+        [dp ^ 1, dp ^ 2, dp ^ 3], hot, onehot, hot_onehot, rows, theirs, got, w_gate, w_up, acc, (scale, hot_scale)
+    )
+
+    def partial(group, hot):
+        own, other = down([dp ^ r for r in group], hot, spread, hot_spread, hidden, hot_hidden, w_down, part)
+        half = own.shape[0] // 2
+        found = []
+        for i in range(len(group)):
+            lanes = slice(i * part, (i + 1) * part)
+            theirs = [swap(other[:half, lanes]), swap(other[half:, lanes])]
+            found.append(own[:, lanes].astype(F32) + jnp.concatenate(theirs, axis=0).astype(F32))
+        return found
+
+    (p3,) = partial((3,), hot)
+    p3 = p3.astype(BF16)
+    hot, p3 = after(hot, p3)
+    corner = across[3](p3)
+    p1, p2 = partial((1, 2), hot)
+    p1, p2 = p1.astype(BF16), p2.astype(BF16)
+    hot, p1, p2, corner = after(hot, p1, p2, corner)
+    by_x, by_y = across[1](p1), across[2](p2)
+    (p0,) = partial((0,), hot)
+    total = p0 + corner.astype(F32) + by_x.astype(F32) + by_y.astype(F32)
+    out = total[(lines - 1) * group_tok :]
+    for i, s in enumerate(order):
+        out = out + along[lines - s](total[i * group_tok : (i + 1) * group_tok].astype(BF16)).astype(F32)
+    return out.astype(BF16)[None]
+
+
 def solution(mesh):
     placed = (
         P("expert", None, None),
@@ -99,6 +548,8 @@
         P("expert", None, "dp"),
         P("expert", "dp", None),
     )
+    n_dp, n_ex = mesh.shape["dp"], mesh.shape["expert"]
+    local = functools.partial(gather_local, n_dp, n_ex) if (n_dp, n_ex) == (4, 8) else dispatch_local
     return jax.shard_map(
         local, mesh=mesh, in_specs=placed, out_specs=P("expert", None, "dp"), check_vma=False
     )

time: 686 us -> 145 us (0.21); the launches traced: 678 us -> 147 us
  waiting for transfers between devices: 321 us -> 44 us
  blocking collectives: 157 us -> 0 us
  matrix products: 79 us -> 0 us
  local copies, waits for them, and re-layouts: 75.5 us -> 6.73 us
  Pallas kernels: 0 us -> 60.2 us
  starting transfers between devices: 5.2 us -> 32.1 us
  other arithmetic: 22 us -> 3.12 us
  between operations: 18.4 us -> 0.38 us
    all_to_all x1 -> x0, waiting for transfers between devices: 201 us -> none  [local(): lax.all_to_all(partial_value.astype(jnp.bfloat16), 'expert', split_axis=0...]
    all_to_all x1 -> x0, blocking collectives: 157 us -> none  [local(): lax.all_to_all(outgoing, 'expert', split_axis=0, concat_axis=0, tiled=True)]
    psum x1 -> x0, waiting for transfers between devices: 97.1 us -> none  [broadcast(): return lax.psum(block, axis)]
    dot_general x4 -> x0, matrix products: 79 us -> none  [the longest x1 51.7 us: local(): jnp.einsum('senf,efm->senm', hidden, w_down, preferred_element_type=jnp.f...]
    pallas_call x0 -> x7, Pallas kernels: none -> 60.2 us  [the longest x2 29.4 us: gate_up(): pl.pallas_call(functools.partial(gate_up_kernel, tuple((len(p) // 2 for p...]
    ppermute x0 -> x30, waiting for transfers between devices: none -> 44 us  [mover(): return lambda x: lax.ppermute(x, AXES, pairs)]
    ppermute x0 -> x30, starting transfers between devices: none -> 32.1 us  [mover(): return lambda x: lax.ppermute(x, AXES, pairs)]
    reduce_scatter x2 -> x0, waiting for transfers between devices: 22.9 us -> none  [the longest x1 22.9 us: local(): lax.psum_scatter(hot_partial.astype(jnp.bfloat16), 'dp', scatter_dimensio...]
  transfers between devices with their start and end apart: 4 -> 30, of which waited for: 3 -> 19; matrix products, arithmetic and copies ran while one was open for 7% -> 3% of each run, Pallas kernels for 0% -> 22%
where the time goes in v2:
time: 145 us; the launch traced here: 147 us
  Pallas kernels  60.2 us (42%)
  waiting for transfers between devices  44 us (30%)
  starting transfers between devices  32.1 us (22%)
  local copies, waits for them, and re-layouts  6.73 us (5%)
  other arithmetic  3.12 us (2%)
    ppermute x30, waiting for transfers between devices, mover(): return lambda x: lax.ppermute(x, AXES, pairs)  44 us
    ppermute x30, starting transfers between devices, mover(): return lambda x: lax.ppermute(x, AXES, pairs)  32.1 us
    pallas_call x2, Pallas kernels, gate_up(): pl.pallas_call(functools.partial(gate_up_kernel, tuple((len(p) // 2 for p...  29.4 us
    pallas_call x3, Pallas kernels, down(): pl.pallas_call(functools.partial(down_kernel, nq), in_specs=[scalars()] *...  24.1 us
    pallas_call x2, Pallas kernels, staged(): pl.pallas_call(functools.partial(staged_kernel, body, len(given), len(inp...  6.7 us
    unnamed x48, local copies, waits for them, and re-layouts  5.29 us
  transfers between devices with their start and end apart: 30, of which 19 were waited for; matrix products, arithmetic and copies ran while one was open for 3% of the time, Pallas kernels for 22%

profile of v2, /device:TPU:0, one launch (start us, length us, event | category | flops | bytes accessed | tf_op | source)
XLA Modules:
  0.0 146.6 jit_solution(17154820563125826591)
XLA Ops:
  3.2 3.7 %collective-permute-start.3 = (bf16[88,1152]{1,0:T(8,128)(2,1)S(1)}, bf16[88,1152]{1,0:T(8,128)(2,1)S(1)}, u32[]{:S(2)}, u32[]{:S(2)}) collective-permute-start(bf16[88,1152]{1,0:T(8,128)(2,1)S(1)} %concatenate.15.refs_0_), channel_id=1, source_target_pairs={{0,4},{1,5},{2,6},{3,7},{4,0},{5,1},{6,2},{7,3},{8,12},{9,13},{10,... | collective-permute-start | bytes 608264 | tf_op jit(solution)/shard_map/ppermute | solution.py:469
  6.9 1.3 collective-permute-start.2
  8.9 8.2 %collective-permute-done.3.refs_3_ = bf16[88,1152]{1,0:T(8,128)(2,1)S(1)} collective-permute-done((bf16[88,1152]{1,0:T(8,128)(2,1)S(1)}, bf16[88,1152]{1,0:T(8,128)(2,1)S(1)}, u32[]{:S(2)}, u32[]{:S(2)}) %collective-permute-start.3) | collective-permute-done | bytes 202784 | tf_op jit(solution)/shard_map/ppermute | solution.py:469
  17.2 5.3 %collective-permute-done.1.refs_1_ = bf16[88,1152]{1,0:T(8,128)(2,1)S(1)} collective-permute-done((bf16[88,1152]{1,0:T(8,128)(2,1)S(1)}, bf16[88,1152]{1,0:T(8,128)(2,1)S(1)}, u32[]{:S(2)}, u32[]{:S(2)}) %collective-permute-start.1) | collective-permute-done | bytes 202784 | tf_op jit(solution)/shard_map/ppermute | solution.py:469
  23.2 2.5 %pack.1 = (bf16[264,1024]{1,0:T(8,128)(2,1)}, bf16[88,1024]{1,0:T(8,128)(2,1)}, bf16[352,128]{1,0:T(8,128)(2,1)}) custom-call(bf16[88,1152]{1,0:T(8,128)(2,1)} %copy-done.7, bf16[88,1152]{1,0:T(8,128)(2,1)} %copy-done.15, bf16[88,1152]{1,0:T(8,128)(2,1)} %copy-done.14, bf16[88,1152]{1,0:T(8,128)(2,1)} %copy-done.13), custom_call_target="tpu_custom_call" | custom-call | bytes 1000000 | tf_op jit(solution)/shard_map/pack/pallas_call | solution.py:133
  25.7 1.6 %collective-permute-start.7 = (bf16[264,1024]{1,0:T(8,128)(2,1)}, bf16[264,1024]{1,0:T(8,128)(2,1)S(1)}, u32[]{:S(2)}, u32[]{:S(2)}) collective-permute-start(bf16[264,1024]{1,0:T(8,128)(2,1)} %get-tuple-element.51.rest_0_), channel_id=1, source_target_pairs={{0,16},{1,17},{2,18},{3,19},{4,20},{5,21},{6,22},{7,23},{8,24},{9,... | collective-permute-start | bytes 1622024 | tf_op jit(solution)/shard_map/ppermute | solution.py:469
  27.3 1.5 %collective-permute-start.6 = (bf16[264,1024]{1,0:T(8,128)(2,1)}, bf16[264,1024]{1,0:T(8,128)(2,1)S(1)}, u32[]{:S(2)}, u32[]{:S(2)}) collective-permute-start(bf16[264,1024]{1,0:T(8,128)(2,1)} %get-tuple-element.51.rest_0_), channel_id=1, source_target_pairs={{0,8},{1,9},{2,10},{3,11},{4,12},{5,13},{6,14},{7,15},{8,0},{9,1},... | collective-permute-start | bytes 1622024 | tf_op jit(solution)/shard_map/ppermute | solution.py:469
  28.8 2.7 %collective-permute-start.9 = (bf16[88,1024]{1,0:T(8,128)(2,1)S(1)}, bf16[88,1024]{1,0:T(8,128)(2,1)S(1)}, u32[]{:S(2)}, u32[]{:S(2)}) collective-permute-start(bf16[88,1024]{1,0:T(8,128)(2,1)S(1)} %get-tuple-element.56), channel_id=1, source_target_pairs={{0,6},{1,7},{2,0},{3,1},{4,2},{5,3},{6,4},{7,5},{8,14},{9,15},{10,... | collective-permute-start | bytes 540680 | tf_op jit(solution)/shard_map/ppermute | solution.py:469
  31.5 2.7 %collective-permute-start.8 = (bf16[88,1024]{1,0:T(8,128)(2,1)S(1)}, bf16[88,1024]{1,0:T(8,128)(2,1)S(1)}, u32[]{:S(2)}, u32[]{:S(2)}) collective-permute-start(bf16[88,1024]{1,0:T(8,128)(2,1)S(1)} %get-tuple-element.56), channel_id=1, source_target_pairs={{0,2},{1,3},{2,4},{3,5},{4,6},{5,7},{6,0},{7,1},{8,10},{9,11},{10,... | collective-permute-start | bytes 540680 | tf_op jit(solution)/shard_map/ppermute | solution.py:469
  34.7 4.2 %places.1 = (bf16[896,704]{1,0:T(8,128)(2,1)}, bf16[240,704]{1,0:T(8,128)(2,1)}, bf16[704,896]{1,0:T(8,128)(2,1)}, bf16[704,240]{1,0:T(8,128)(2,1)}, f32[8,112,1...) custom-call(s32[1]{0:T(128)} %bitcast.1.refs_0_, bf16[352,128]{1,0:T(8,128)(2,1)} %get-tuple-element.46.refs_1_, ...), custom_call_target="tpu_custom_call" | custom-call | bytes 15000000 | tf_op jit(solution)/shard_map/places/pallas_call | solution.py:133
  39.0 9.7 %gate_up.2 = (f32[8,112,768]{2,1,0:T(8,128)}, f32[240,768]{1,0:T(8,128)}) custom-call(s32[1]{0:T(128)} %bitcast.quarter, s32[1]{0:T(128)} %get-tuple-element.75.busy, bf16[8,4096,384]{2,1,0:T(8,128)(2,1)} %wg.3, bf16[8,4096,384]{2,1,0:T(8,128)(2,1)} %wu.3, bf16[88,4096]{1,0:T(8,128)(2,1)} %bitcast.22, bf16[88,4096]{1,0:T(8,128)(2,1)} %copy-done.6, ...), custom_call_target="tpu_custom_call" | custom-call | tf_op jit(solution)/shard_map/gate_up/pallas_call | solution.py:356
  50.5 1.3 collective-permute-done.13.rest_7_
  53.4 19.8 %gate_up.3 = (bf16[8,112,384]{2,1,0:T(8,128)(2,1)}, bf16[240,384]{1,0:T(8,128)(2,1)}) custom-call(s32[3]{0:T(128)} %pad_add_fusion.quarter, s32[1]{0:T(128)} %get-tuple-element.75.busy, bf16[8,4096,384]{2,1,0:T(8,128)(2,1)} %wg.3, bf16[8,4096,384]{2,1,0:T(8,128)(2,1)} %wu.3, bf16[88,4096]{1,0:T(8,128)(2,1)} %bitcast.23, bf16[88,4096]{1,0:T(8,128)(2,1)} %copy-done.6, ...), custom_call_target="tpu_custom_call" | custom-call | tf_op jit(solution)/shard_map/gate_up/pallas_call | solution.py:356
  75.2 6.4 %down.3 = (bf16[352,1024]{1,0:T(8,128)(2,1)S(1)}, bf16[352,1024]{1,0:T(8,128)(2,1)S(1)}) custom-call(s32[1]{0:T(128)} %bitcast.6.quarter, s32[1]{0:T(128)} %get-tuple-element.75.busy, bf16[704,896]{1,0:T(8,128)(2,1)S(1)} %copy-done, bf16[704,240]{1,0:T(8,128)(2,1)S(1)} %copy-done.3, bf16[8,112,384]{2,1,0:T(8,128)(2,1)S(1)} %copy-done.1, ...), custom_call_target="tpu_custom_call" | custom-call | tf_op jit(solution)/shard_map/down/pallas_call | solution.py:441
  84.2 2.5 %collective-permute-start.22 = (bf16[352,1024]{1,0:T(8,128)(2,1)S(1)}, bf16[352,1024]{1,0:T(8,128)(2,1)S(1)}, u32[]{:S(2)}, u32[]{:S(2)}) collective-permute-start(bf16[352,1024]{1,0:T(8,128)(2,1)S(1)} %add_convert_fusion.2), channel_id=1, source_target_pairs={{0,24},{1,25},{2,26},{3,27},{4,28},{5,29},{6,30},{7,31},{8,16},{9,... | collective-permute-start | bytes 2162696 | tf_op jit(solution)/shard_map/ppermute | solution.py:469
  86.7 11.3 %down.4 = (bf16[352,2048]{1,0:T(8,128)(2,1)S(1)}, bf16[352,2048]{1,0:T(8,128)(2,1)S(1)}) custom-call(s32[2]{0:T(128)S(1)} %pad_add_fusion.1.quarter, s32[1]{0:T(128)} %get-tuple-element.75.busy, bf16[704,896]{1,0:T(8,128)(2,1)S(1)} %copy-done, bf16[704,240]{1,0:T(8,128)(2,1)S(1)} %copy-done.3, bf16[8,112,384]{2,1,0:T(8,128)(2,1)S(1)} %copy-done.1, ...), custom_call_target="tpu_custom_call" | custom-call | tf_op jit(solution)/shard_map/down/pallas_call | solution.py:441
  103.3 1.5 %collective-permute-start.25 = (bf16[352,1024]{1,0:T(8,128)(2,1)S(1)}, bf16[352,1024]{1,0:T(8,128)(2,1)S(1)}, u32[]{:S(2)}, u32[]{:S(2)}) collective-permute-start(bf16[352,1024]{1,0:T(8,128)(2,1)S(1)} %get-tuple-element.79), channel_id=1, source_target_pairs={{0,8},{1,9},{2,10},{3,11},{4,12},{5,13},{6,14},{7,15},{8,0},{9,1},... | collective-permute-start | bytes 2162696 | tf_op jit(solution)/shard_map/ppermute | solution.py:469
  104.8 1.5 %collective-permute-start.26 = (bf16[352,1024]{1,0:T(8,128)(2,1)S(1)}, bf16[352,1024]{1,0:T(8,128)(2,1)S(1)}, u32[]{:S(2)}, u32[]{:S(2)}) collective-permute-start(bf16[352,1024]{1,0:T(8,128)(2,1)S(1)} %get-tuple-element.80), channel_id=1, source_target_pairs={{0,16},{1,17},{2,18},{3,19},{4,20},{5,21},{6,22},{7,23},{8,24},{9,... | collective-permute-start | bytes 2162696 | tf_op jit(solution)/shard_map/ppermute | solution.py:469
  106.3 6.4 %down.5 = (bf16[352,1024]{1,0:T(8,128)(2,1)S(1)}, bf16[352,1024]{1,0:T(8,128)(2,1)S(1)}) custom-call(s32[1]{0:T(128)} %bitcast.quarter, s32[1]{0:T(128)} %get-tuple-element.75.busy, bf16[704,896]{1,0:T(8,128)(2,1)S(1)} %copy-done, bf16[704,240]{1,0:T(8,128)(2,1)S(1)} %copy-done.3, bf16[8,112,384]{2,1,0:T(8,128)(2,1)S(1)} %copy-done.2, ...), custom_call_target="tpu_custom_call" | custom-call | tf_op jit(solution)/shard_map/down/pallas_call | solution.py:441
  115.1 5.6 %collective-permute-done.25 = bf16[352,1024]{1,0:T(8,128)(2,1)S(1)} collective-permute-done((bf16[352,1024]{1,0:T(8,128)(2,1)S(1)}, bf16[352,1024]{1,0:T(8,128)(2,1)S(1)}, u32[]{:S(2)}, u32[]{:S(2)}) %collective-permute-start.25) | collective-permute-done | bytes 720928 | tf_op jit(solution)/shard_map/ppermute | solution.py:469
  122.7 2.0 %collective-permute-start.27 = (bf16[88,1024]{1,0:T(8,128)(2,1)S(1)}, bf16[88,1024]{1,0:T(8,128)(2,1)S(1)}, u32[]{:S(2)}, u32[]{:S(2)}) collective-permute-start(bf16[88,1024]{1,0:T(8,128)(2,1)S(1)} %get-tuple-element.89), channel_id=1, source_target_pairs={{0,6},{1,7},{2,0},{3,1},{4,2},{5,3},{6,4},{7,5},{8,14},{9,15},{10,... | collective-permute-start | bytes 540680 | tf_op jit(solution)/shard_map/ppermute | solution.py:469
  124.7 6.0 %collective-permute-start.29 = (bf16[88,1024]{1,0:T(8,128)(2,1)S(1)}, bf16[88,1024]{1,0:T(8,128)(2,1)S(1)}, u32[]{:S(2)}, u32[]{:S(2)}) collective-permute-start(bf16[88,1024]{1,0:T(8,128)(2,1)S(1)} %get-tuple-element.90), channel_id=1, source_target_pairs={{0,4},{1,5},{2,6},{3,7},{4,0},{5,1},{6,2},{7,3},{8,12},{9,13},{10,... | collective-permute-start | bytes 540680 | tf_op jit(solution)/shard_map/ppermute | solution.py:469
  130.7 2.3 %collective-permute-done.27 = bf16[88,1024]{1,0:T(8,128)(2,1)S(1)} collective-permute-done((bf16[88,1024]{1,0:T(8,128)(2,1)S(1)}, bf16[88,1024]{1,0:T(8,128)(2,1)S(1)}, u32[]{:S(2)}, u32[]{:S(2)}) %collective-permute-start.27) | collective-permute-done | bytes 180256 | tf_op jit(solution)/shard_map/ppermute | solution.py:469
  133.0 12.8 %collective-permute-done.29 = bf16[88,1024]{1,0:T(8,128)(2,1)S(1)} collective-permute-done((bf16[88,1024]{1,0:T(8,128)(2,1)S(1)}, bf16[88,1024]{1,0:T(8,128)(2,1)S(1)}, u32[]{:S(2)}, u32[]{:S(2)}) %collective-permute-start.29) | collective-permute-done | bytes 180256 | tf_op jit(solution)/shard_map/ppermute | solution.py:469
  (106 shorter events, 23.4 us)
Async XLA Ops:
  0.0 22.5 %collective-permute-start = (bf16[88,4096]{1,0:T(8,128)(2,1)}, bf16[88,4096]{1,0:T(8,128)(2,1)S(1)}, u32[]{:S(2)}, u32[]{:S(2)}) collective-permute-start(bf16[88,4096]{1,0:T(8,128)(2,1)} %bitcast.21), channel_id=1, source_target_pairs={{0,1},{1,0},{2,3},{3,2},{4,5},{5,4},{6,7},{7,6},{8,9},{9,8},{10,11... | collective-permute-start | bytes 2162696 | tf_op jit(solution)/shard_map/ppermute | solution.py:469
  3.2 13.9 %collective-permute-start.3 = (bf16[88,1152]{1,0:T(8,128)(2,1)S(1)}, bf16[88,1152]{1,0:T(8,128)(2,1)S(1)}, u32[]{:S(2)}, u32[]{:S(2)}) collective-permute-start(bf16[88,1152]{1,0:T(8,128)(2,1)S(1)} %concatenate.15.refs_0_), channel_id=1, source_target_pairs={{0,4},{1,5},{2,6},{3,7},{4,0},{5,1},{6,2},{7,3},{8,12},{9,13},{10,... | collective-permute-start | bytes 608264 | tf_op jit(solution)/shard_map/ppermute | solution.py:469
  6.9 10.3 %collective-permute-start.2 = (bf16[88,1152]{1,0:T(8,128)(2,1)S(1)}, bf16[88,1152]{1,0:T(8,128)(2,1)S(1)}, u32[]{:S(2)}, u32[]{:S(2)}) collective-permute-start(bf16[88,1152]{1,0:T(8,128)(2,1)S(1)} %concatenate.15.refs_0_), channel_id=1, source_target_pairs={{0,6},{1,7},{2,0},{3,1},{4,2},{5,3},{6,4},{7,5},{8,14},{9,15},{10,... | collective-permute-start | bytes 608264 | tf_op jit(solution)/shard_map/ppermute | solution.py:469
  8.2 14.3 %collective-permute-start.1 = (bf16[88,1152]{1,0:T(8,128)(2,1)S(1)}, bf16[88,1152]{1,0:T(8,128)(2,1)S(1)}, u32[]{:S(2)}, u32[]{:S(2)}) collective-permute-start(bf16[88,1152]{1,0:T(8,128)(2,1)S(1)} %concatenate.15.refs_0_), channel_id=1, source_target_pairs={{0,2},{1,3},{2,4},{3,5},{4,6},{5,7},{6,0},{7,1},{8,10},{9,11},{10,... | collective-permute-start | bytes 608264 | tf_op jit(solution)/shard_map/ppermute | solution.py:469
  25.7 8.6 %collective-permute-start.5 = (bf16[264,1024]{1,0:T(8,128)(2,1)}, bf16[264,1024]{1,0:T(8,128)(2,1)S(1)}, u32[]{:S(2)}, u32[]{:S(2)}) collective-permute-start(bf16[264,1024]{1,0:T(8,128)(2,1)} %get-tuple-element.51.rest_0_), channel_id=1, source_target_pairs={{0,1},{1,0},{2,3},{3,2},{4,5},{5,4},{6,7},{7,6},{8,9},{9,8},{10,11... | collective-permute-start | bytes 1622024 | tf_op jit(solution)/shard_map/ppermute | solution.py:469
  25.7 23.0 %collective-permute-start.7 = (bf16[264,1024]{1,0:T(8,128)(2,1)}, bf16[264,1024]{1,0:T(8,128)(2,1)S(1)}, u32[]{:S(2)}, u32[]{:S(2)}) collective-permute-start(bf16[264,1024]{1,0:T(8,128)(2,1)} %get-tuple-element.51.rest_0_), channel_id=1, source_target_pairs={{0,16},{1,17},{2,18},{3,19},{4,20},{5,21},{6,22},{7,23},{8,24},{9,... | collective-permute-start | bytes 1622024 | tf_op jit(solution)/shard_map/ppermute | solution.py:469
  27.3 21.4 %collective-permute-start.6 = (bf16[264,1024]{1,0:T(8,128)(2,1)}, bf16[264,1024]{1,0:T(8,128)(2,1)S(1)}, u32[]{:S(2)}, u32[]{:S(2)}) collective-permute-start(bf16[264,1024]{1,0:T(8,128)(2,1)} %get-tuple-element.51.rest_0_), channel_id=1, source_target_pairs={{0,8},{1,9},{2,10},{3,11},{4,12},{5,13},{6,14},{7,15},{8,0},{9,1},... | collective-permute-start | bytes 1622024 | tf_op jit(solution)/shard_map/ppermute | solution.py:469
  28.8 2.7 %collective-permute-start.4 = (bf16[352,128]{1,0:T(8,128)(2,1)}, bf16[352,128]{1,0:T(8,128)(2,1)S(1)}, u32[]{:S(2)}, u32[]{:S(2)}) collective-permute-start(bf16[352,128]{1,0:T(8,128)(2,1)} %get-tuple-element.46.refs_1_), channel_id=1, source_target_pairs={{0,1},{1,0},{2,3},{3,2},{4,5},{5,4},{6,7},{7,6},{8,9},{9,8},{10,11... | collective-permute-start | bytes 270344 | tf_op jit(solution)/shard_map/ppermute | solution.py:469
  28.8 19.9 %collective-permute-start.9 = (bf16[88,1024]{1,0:T(8,128)(2,1)S(1)}, bf16[88,1024]{1,0:T(8,128)(2,1)S(1)}, u32[]{:S(2)}, u32[]{:S(2)}) collective-permute-start(bf16[88,1024]{1,0:T(8,128)(2,1)S(1)} %get-tuple-element.56), channel_id=1, source_target_pairs={{0,6},{1,7},{2,0},{3,1},{4,2},{5,3},{6,4},{7,5},{8,14},{9,15},{10,... | collective-permute-start | bytes 540680 | tf_op jit(solution)/shard_map/ppermute | solution.py:469
  31.5 17.2 %collective-permute-start.8 = (bf16[88,1024]{1,0:T(8,128)(2,1)S(1)}, bf16[88,1024]{1,0:T(8,128)(2,1)S(1)}, u32[]{:S(2)}, u32[]{:S(2)}) collective-permute-start(bf16[88,1024]{1,0:T(8,128)(2,1)S(1)} %get-tuple-element.56), channel_id=1, source_target_pairs={{0,2},{1,3},{2,4},{3,5},{4,6},{5,7},{6,0},{7,1},{8,10},{9,11},{10,... | collective-permute-start | bytes 540680 | tf_op jit(solution)/shard_map/ppermute | solution.py:469
  34.3 14.5 %collective-permute-start.10 = (bf16[88,1024]{1,0:T(8,128)(2,1)}, bf16[88,1024]{1,0:T(8,128)(2,1)S(1)}, u32[]{:S(2)}, u32[]{:S(2)}) collective-permute-start(bf16[88,1024]{1,0:T(8,128)(2,1)} %get-tuple-element.57), channel_id=1, source_target_pairs={{0,24},{1,25},{2,26},{3,27},{4,28},{5,29},{6,30},{7,31},{8,16},{9,... | collective-permute-start | bytes 540680 | tf_op jit(solution)/shard_map/ppermute | solution.py:469
  48.8 3.6 %collective-permute-start.11 = (bf16[264,1024]{1,0:T(8,128)(2,1)S(1)}, bf16[264,1024]{1,0:T(8,128)(2,1)S(1)}, u32[]{:S(2)}, u32[]{:S(2)}) collective-permute-start(bf16[264,1024]{1,0:T(8,128)(2,1)S(1)} %collective-permute-done.6.rest_0_), channel_id=1, source_target_pairs={{0,1},{1,0},{2,3},{3,2},{4,5},{5,4},{6,7},{7,6},{8,9},{9,8},{10,11... | collective-permute-start | bytes 1622024 | tf_op jit(solution)/shard_map/ppermute | solution.py:469
  48.9 3.5 %collective-permute-start.12 = (bf16[264,1024]{1,0:T(8,128)(2,1)S(1)}, bf16[264,1024]{1,0:T(8,128)(2,1)S(1)}, u32[]{:S(2)}, u32[]{:S(2)}) collective-permute-start(bf16[264,1024]{1,0:T(8,128)(2,1)S(1)} %collective-permute-done.7.rest_2_), channel_id=1, source_target_pairs={{0,1},{1,0},{2,3},{3,2},{4,5},{5,4},{6,7},{7,6},{8,9},{9,8},{10,11... | collective-permute-start | bytes 1622024 | tf_op jit(solution)/shard_map/ppermute | solution.py:469
  49.4 2.5 %collective-permute-start.13 = (bf16[88,1024]{1,0:T(8,128)(2,1)S(1)}, bf16[88,1024]{1,0:T(8,128)(2,1)S(1)}, u32[]{:S(2)}, u32[]{:S(2)}) collective-permute-start(bf16[88,1024]{1,0:T(8,128)(2,1)S(1)} %collective-permute-done.8.rest_4_), channel_id=1, source_target_pairs={{0,1},{1,0},{2,3},{3,2},{4,5},{5,4},{6,7},{7,6},{8,9},{9,8},{10,11... | collective-permute-start | bytes 540680 | tf_op jit(solution)/shard_map/ppermute | solution.py:469
  49.4 2.6 %collective-permute-start.14 = (bf16[88,1024]{1,0:T(8,128)(2,1)S(1)}, bf16[88,1024]{1,0:T(8,128)(2,1)S(1)}, u32[]{:S(2)}, u32[]{:S(2)}) collective-permute-start(bf16[88,1024]{1,0:T(8,128)(2,1)S(1)} %collective-permute-done.9.rest_5_), channel_id=1, source_target_pairs={{0,1},{1,0},{2,3},{3,2},{4,5},{5,4},{6,7},{7,6},{8,9},{9,8},{10,11... | collective-permute-start | bytes 540680 | tf_op jit(solution)/shard_map/ppermute | solution.py:469
  49.9 2.5 %collective-permute-start.15 = (bf16[88,1024]{1,0:T(8,128)(2,1)S(1)}, bf16[88,1024]{1,0:T(8,128)(2,1)S(1)}, u32[]{:S(2)}, u32[]{:S(2)}) collective-permute-start(bf16[88,1024]{1,0:T(8,128)(2,1)S(1)} %collective-permute-done.10.rest_6_), channel_id=1, source_target_pairs={{0,1},{1,0},{2,3},{3,2},{4,5},{5,4},{6,7},{7,6},{8,9},{9,8},{10,11... | collective-permute-start | bytes 540680 | tf_op jit(solution)/shard_map/ppermute | solution.py:469
  84.2 19.1 %collective-permute-start.22 = (bf16[352,1024]{1,0:T(8,128)(2,1)S(1)}, bf16[352,1024]{1,0:T(8,128)(2,1)S(1)}, u32[]{:S(2)}, u32[]{:S(2)}) collective-permute-start(bf16[352,1024]{1,0:T(8,128)(2,1)S(1)} %add_convert_fusion.2), channel_id=1, source_target_pairs={{0,24},{1,25},{2,26},{3,27},{4,28},{5,29},{6,30},{7,31},{8,16},{9,... | collective-permute-start | bytes 2162696 | tf_op jit(solution)/shard_map/ppermute | solution.py:469
  98.7 2.2 %collective-permute-start.19 = (bf16[176,1024]{1,0:T(8,128)(2,1)S(1)}, bf16[176,1024]{1,0:T(8,128)(2,1)S(1)}, u32[]{:S(2)}, u32[]{:S(2)}) collective-permute-start(bf16[176,1024]{1,0:T(8,128)(2,1)S(1)} %get-tuple-element.87), channel_id=1, source_target_pairs={{0,1},{1,0},{2,3},{3,2},{4,5},{5,4},{6,7},{7,6},{8,9},{9,8},{10,11... | collective-permute-start | bytes 1081352 | tf_op jit(solution)/shard_map/ppermute | solution.py:469
  98.8 2.6 %collective-permute-start.18 = (bf16[176,1024]{1,0:T(8,128)(2,1)S(1)}, bf16[176,1024]{1,0:T(8,128)(2,1)S(1)}, u32[]{:S(2)}, u32[]{:S(2)}) collective-permute-start(bf16[176,1024]{1,0:T(8,128)(2,1)S(1)} %get-tuple-element.88), channel_id=1, source_target_pairs={{0,1},{1,0},{2,3},{3,2},{4,5},{5,4},{6,7},{7,6},{8,9},{9,8},{10,11... | collective-permute-start | bytes 1081352 | tf_op jit(solution)/shard_map/ppermute | solution.py:469
  103.3 17.4 %collective-permute-start.25 = (bf16[352,1024]{1,0:T(8,128)(2,1)S(1)}, bf16[352,1024]{1,0:T(8,128)(2,1)S(1)}, u32[]{:S(2)}, u32[]{:S(2)}) collective-permute-start(bf16[352,1024]{1,0:T(8,128)(2,1)S(1)} %get-tuple-element.79), channel_id=1, source_target_pairs={{0,8},{1,9},{2,10},{3,11},{4,12},{5,13},{6,14},{7,15},{8,0},{9,1},... | collective-permute-start | bytes 2162696 | tf_op jit(solution)/shard_map/ppermute | solution.py:469
  104.8 17.1 %collective-permute-start.26 = (bf16[352,1024]{1,0:T(8,128)(2,1)S(1)}, bf16[352,1024]{1,0:T(8,128)(2,1)S(1)}, u32[]{:S(2)}, u32[]{:S(2)}) collective-permute-start(bf16[352,1024]{1,0:T(8,128)(2,1)S(1)} %get-tuple-element.80), channel_id=1, source_target_pairs={{0,16},{1,17},{2,18},{3,19},{4,20},{5,21},{6,22},{7,23},{8,24},{9,... | collective-permute-start | bytes 2162696 | tf_op jit(solution)/shard_map/ppermute | solution.py:469
  122.7 10.3 %collective-permute-start.27 = (bf16[88,1024]{1,0:T(8,128)(2,1)S(1)}, bf16[88,1024]{1,0:T(8,128)(2,1)S(1)}, u32[]{:S(2)}, u32[]{:S(2)}) collective-permute-start(bf16[88,1024]{1,0:T(8,128)(2,1)S(1)} %get-tuple-element.89), channel_id=1, source_target_pairs={{0,6},{1,7},{2,0},{3,1},{4,2},{5,3},{6,4},{7,5},{8,14},{9,15},{10,... | collective-permute-start | bytes 540680 | tf_op jit(solution)/shard_map/ppermute | solution.py:469
  124.7 21.1 %collective-permute-start.29 = (bf16[88,1024]{1,0:T(8,128)(2,1)S(1)}, bf16[88,1024]{1,0:T(8,128)(2,1)S(1)}, u32[]{:S(2)}, u32[]{:S(2)}) collective-permute-start(bf16[88,1024]{1,0:T(8,128)(2,1)S(1)} %get-tuple-element.90), channel_id=1, source_target_pairs={{0,4},{1,5},{2,6},{3,7},{4,0},{5,1},{6,2},{7,3},{8,12},{9,13},{10,... | collective-permute-start | bytes 540680 | tf_op jit(solution)/shard_map/ppermute | solution.py:469
  130.7 15.1 %collective-permute-start.28 = (bf16[88,1024]{1,0:T(8,128)(2,1)S(1)}, bf16[88,1024]{1,0:T(8,128)(2,1)S(1)}, u32[]{:S(2)}, u32[]{:S(2)}) collective-permute-start(bf16[88,1024]{1,0:T(8,128)(2,1)S(1)} %get-tuple-element.91), channel_id=1, source_target_pairs={{0,2},{1,3},{2,4},{3,5},{4,6},{5,7},{6,0},{7,1},{8,10},{9,11},{10,... | collective-permute-start | bytes 540680 | tf_op jit(solution)/shard_map/ppermute | solution.py:469
  (29 other events, 141.5 us)

commit v3 on v2

--- a/solution.py
+++ b/solution.py
@@ -223,15 +223,21 @@
         taken, rest[:count] = rest[:count], []
         return taken
 
+    if last:
+        spread_far, hot_far, wd = take(3)
     far = [take(2 * count) for count in counts]
     loaded = take(2 + (0 if first else 2) + (2 if last else 0))
     out, hout = take(2)
+    if last:
+        own_sum, *other_sum = take(3)
     near_v = [take(2 * count) for count in counts]
     loaded_v = take(len(loaded))
     onehot, hot_onehot = loaded_v[:2]
     prev, hprev = (None, None) if first else loaded_v[2:4]
     scale, hscale = loaded_v[-2:] if last else (None, None)
-    total, htotal = (out, hout) if last else take(2)
+    total, htotal = take(2)
+    if last:
+        spread, hot_spread, y, yh, held_d, down_sem, spread_sem = take(7)
     own, x, xg, xh, held, sem, load_sem, far_sem, own_sem, out_sem = rest
     n, _, f = wg.shape
     rows = xg.shape[1]
@@ -267,8 +273,8 @@
         for copy in copies:
             copy.start()
 
-    start(loads[:2] + pieces[0])
-    ahead = [copies(e, e) for e in range(min(depth, n))]
+    start(loads[:2] + pieces[0] + copies(0, 0))
+    ahead = [copies(e, e) for e in range(1, min(depth, n))]
     ahead = [sum(pieces[1:], [])] + ahead[:1] + [loads[2:]] + ahead[1:]
     for i in range(nq):
         lanes = slice(i * part, (i + 1) * part)
@@ -304,6 +310,9 @@
             dst[low] = g
             dst[high] = u
 
+    def down_copy(e):
+        return pltpu.make_async_copy(wd.at[e, :, pl.ds(start_of(nq - 1), part)], held_d.at[e], down_sem.at[e])
+
     def store(e):
         return pltpu.make_async_copy(total.at[e], out.at[e], out_sem.at[e])
 
@@ -324,18 +333,36 @@
             for copy in copies(e + depth, slot):
                 copy.start()
 
-        if not last:
-            store(e).start()
-
-    if not last:
-        tail = pltpu.make_async_copy(htotal, hout, out_sem.at[n])
-        tail.start()
-        for e in range(n):
-            store(e).wait()
-        tail.wait()
-
-
-def gate_up(quarters, hot, onehot, hot_onehot, mine, theirs, got, w_gate, w_up, acc, scales):
+        if last:
+
+            @pl.when(e >= n - depth)
+            def _():
+                for i in range(2):
+                    down_copy((e - (n - depth)) * 2 + i).start()
+
+        store(e).start()
+
+    tail = pltpu.make_async_copy(htotal, hout, out_sem.at[n])
+    tail.start()
+    if last:
+        pairs = (spread_far, spread), (hot_far, hot_spread)
+        spreads = [pltpu.make_async_copy(s, d, spread_sem.at[k]) for k, (s, d) in enumerate(pairs)]
+        start(spreads)
+
+        def ready():
+            for copy in spreads:
+                copy.wait()
+
+        down_step(
+            total, htotal, held_d, hot, spread, hot_spread, y, yh, lambda e: down_copy(e).wait(), ready,
+            lambda value: put_sums(value, own_sum, *other_sum),
+        )
+    for e in range(n):
+        store(e).wait()
+    tail.wait()
+
+
+def gate_up(quarters, hot, onehot, hot_onehot, mine, theirs, got, w_gate, w_up, acc, scales, spreads, w_down):
     n, width, f = w_gate.shape
     tok = onehot.shape[1]
     part = got[0][0].shape[1]
@@ -346,17 +373,29 @@
     depth = min(n, 4)
     loaded = [onehot, hot_onehot] + ([] if first else list(acc)) + list(scales or ())
     far = [piece for pieces in got for piece in pieces]
-    operands = [jnp.stack(quarters).astype(jnp.int32), hot, w_gate, w_up, mine, theirs] + far + loaded
+    operands = [jnp.stack(quarters).astype(jnp.int32), hot, w_gate, w_up, mine, theirs]
+    operands += ([*spreads, w_down] if last else []) + far + loaded
     specs = [scalars()] * 2 + [outside()] * (len(operands) - 2)
     if last:
         outs = (jax.ShapeDtypeStruct((n, rows, f), BF16), jax.ShapeDtypeStruct((hrows, f), BF16))
     else:
         outs = (jax.ShapeDtypeStruct((n, rows, 2 * f), F32), jax.ShapeDtypeStruct((hrows, 2 * f), F32))
-    scratch = [] if last else [pltpu.VMEM(o.shape, o.dtype) for o in outs]
+    scratch = [pltpu.VMEM(o.shape, o.dtype) for o in outs]
+    out_specs = (outside(),) * 2
+    if last:
+        outs += sums_of(tok, part)
+        out_specs += (inside(),) * 3
+        scratch += [pltpu.VMEM(a.shape, BF16) for a in spreads] + [
+            pltpu.VMEM((n * rows, part), BF16),
+            pltpu.VMEM((hrows, part), BF16),
+            pltpu.VMEM((n, f, part), BF16),
+            pltpu.SemaphoreType.DMA((n,)),
+            pltpu.SemaphoreType.DMA((2,)),
+        ]
     return pl.pallas_call(
         functools.partial(gate_up_kernel, tuple(len(p) // 2 for p in got), first, last, depth),
         in_specs=specs,
-        out_specs=(inside(), inside()) if last else (outside(), outside()),
+        out_specs=out_specs,
         out_shape=outs,
         scratch_shapes=[pltpu.VMEM(a.shape, a.dtype) for a in far + loaded]
         + scratch
@@ -380,10 +419,46 @@
     )(*operands)
 
 
-def down_kernel(nq, quarter, busy, spread_far, hot_far, hidden, hhidden, wd, out_a, out_b, *scratch):
-    spread, hot_spread, y, yh, held, sem, load_sem = scratch
+def sums_of(tok, part):
+    return tuple(jax.ShapeDtypeStruct((tok // count, part), BF16) for count in (2, 4, 4))
+
+
+def put_sums(value, own, *other):
+    half = own.shape[0]
+    own[...] = value[:half]
+    for i, piece in enumerate(other):
+        at = half + i * piece.shape[0]
+        piece[...] = value[at : at + piece.shape[0]]
+
+
+def down_step(hidden, hhidden, held, hot, spread, hot_spread, y, yh, before, ready, put):
     n, rows, _ = hidden.shape
-    half = out_a.shape[0]
+    @pl.loop(0, n)
+    def _(e):
+        before(e)
+        at = pl.multiple_of(e * rows, 16)
+        y[pl.ds(at, rows), :] = jnp.dot(hidden[e], held[e], preferred_element_type=F32).astype(BF16)
+
+    @pl.when(hot >= 0)
+    def _():
+        yh[...] = jnp.dot(hhidden[...], held[hot], preferred_element_type=F32).astype(BF16)
+
+    ready()
+
+    @pl.when(hot < 0)
+    def _():
+        put(jnp.dot(spread[...], y[...], preferred_element_type=F32).astype(BF16))
+
+    @pl.when(hot >= 0)
+    def _():
+        value = jnp.dot(spread[...], y[...], preferred_element_type=F32)
+        put((value + jnp.dot(hot_spread[...], yh[...], preferred_element_type=F32)).astype(BF16))
+
+
+def down_kernel(nq, quarter, busy, spread_far, hot_far, hidden_far, hhidden_far, wd, *rest):
+    outs, scratch = rest[: 3 * nq], rest[3 * nq :]
+    spread, hot_spread, hidden, hhidden, y, yh, total, held, sem, load_sem = scratch
+    n, rows, _ = hidden.shape
     part = y.shape[1]
     hot = busy[0]
 
@@ -391,44 +466,45 @@
         column = pl.ds(pl.multiple_of(quarter[i] * part, part), part)
         return pltpu.make_async_copy(wd.at[e, :, column], held.at[i, e], sem.at[i, e])
 
-    pairs = (spread_far, spread), (hot_far, hot_spread)
+    pairs = (hidden_far, hidden), (hhidden_far, hhidden), (spread_far, spread), (hot_far, hot_spread)
     loads = [pltpu.make_async_copy(s, d, load_sem.at[k]) for k, (s, d) in enumerate(pairs)]
-    steps = [(i, e) for i in range(nq) for e in range(n)]
-    window = 6
-    for step in steps[:window]:
-        copy(*step).start()
-
-    for i in range(nq):
-        lanes = slice(i * part, (i + 1) * part)
-        for e in range(n):
+    steps, window = nq * n, 6
+    loads[0].start()
+    for e in range(window):
+        copy(0, e).start()
+    for load in loads[1:]:
+        load.start()
+    loads[0].wait()
+
+    @pl.loop(0, nq)
+    def _(i):
+        def before(e):
             copy(i, e).wait()
-            for step in steps[i * n + e + window : i * n + e + window + 1]:
-                copy(*step).start()
-            if i == 0 and e < 2:
-                loads[e].start()
-            y[e * rows : (e + 1) * rows, :] = jnp.dot(hidden[e], held[i, e], preferred_element_type=F32).astype(BF16)
-
-        @pl.when(hot >= 0)
-        def _():
-            yh[...] = jnp.dot(hhidden[...], held[i, hot], preferred_element_type=F32).astype(BF16)
-
-        if i == 0:
-            for load in loads:
-                load.wait()
-
-        @pl.when(hot < 0)
-        def _():
-            value = jnp.dot(spread[...], y[...], preferred_element_type=F32).astype(BF16)
-            out_a[:, lanes] = value[:half]
-            out_b[:, lanes] = value[half:]
-
-        @pl.when(hot >= 0)
-        def _():
-            value = jnp.dot(spread[...], y[...], preferred_element_type=F32)
-            value = value + jnp.dot(hot_spread[...], yh[...], preferred_element_type=F32)
-            value = value.astype(BF16)
-            out_a[:, lanes] = value[:half]
-            out_b[:, lanes] = value[half:]
+            ahead = i * n + e + window
+
+            @pl.when(ahead < steps)
+            def _():
+                copy(lax.div(ahead, n), lax.rem(ahead, n)).start()
+
+            @pl.when((i == 0) & (e == 0))
+            def _():
+                loads[1].wait()
+
+        def ready():
+            @pl.when(i == 0)
+            def _():
+                loads[2].wait()
+                loads[3].wait()
+
+        def put_this(value):
+            total[...] = value
+            for q in range(nq):
+
+                @pl.when(i == q)
+                def _(q=q):
+                    put_sums(total, *outs[3 * q : 3 * q + 3])
+
+        down_step(hidden, hhidden, held.at[i], hot, spread, hot_spread, y, yh, before, ready, put_this)
 
 
 def down(quarters, hot, spread, hot_spread, hidden, hhidden, w_down, part):
@@ -437,20 +513,23 @@
     rows = hidden.shape[1]
     hrows = hhidden.shape[0]
     nq = len(quarters)
-    out = jax.ShapeDtypeStruct((tok // 2, nq * part), BF16)
+    outs = sums_of(tok, part) * nq
     return pl.pallas_call(
         functools.partial(down_kernel, nq),
-        in_specs=[scalars()] * 2 + [outside()] * 2 + [inside()] * 2 + [outside()],
-        out_specs=(inside(), inside()),
-        out_shape=(out, out),
+        in_specs=[scalars()] * 2 + [outside()] * 5,
+        out_specs=(inside(),) * len(outs),
+        out_shape=outs,
         scratch_shapes=[
             pltpu.VMEM(spread.shape, BF16),
             pltpu.VMEM(hot_spread.shape, BF16),
+            pltpu.VMEM(hidden.shape, BF16),
+            pltpu.VMEM(hhidden.shape, BF16),
             pltpu.VMEM((n * rows, part), BF16),
             pltpu.VMEM((hrows, part), BF16),
+            pltpu.VMEM((tok, part), BF16),
             pltpu.VMEM((nq, n, f, part), BF16),
             pltpu.SemaphoreType.DMA((nq, n)),
-            pltpu.SemaphoreType.DMA((2,)),
+            pltpu.SemaphoreType.DMA((4,)),
         ],
         compiler_params=pltpu.CompilerParams(vmem_limit_bytes=46 * 1024 * 1024),
         cost_estimate=pl.CostEstimate(
@@ -506,36 +585,41 @@
     onehot, hot_onehot, spread, hot_spread, scale, hot_scale, hot = places(
         (me * n).astype(jnp.int32)[None], table, table_other, n, n_ex, top_k
     )
-    acc = gate_up([dp], hot, onehot, hot_onehot, rows, theirs, [[near, near_other]], w_gate, w_up, None, None)
+    acc = gate_up([dp], hot, onehot, hot_onehot, rows, theirs, [[near, near_other]], w_gate, w_up, None, None, None, None)
     acc, by_x, by_y, corner = after(acc, by_x, by_y, corner)
     got = [list(pieces) + [swap(piece) for piece in pieces] for pieces in ((by_x,), (by_y,), corner)]
-    hidden, hot_hidden = gate_up(
-        [dp ^ 1, dp ^ 2, dp ^ 3], hot, onehot, hot_onehot, rows, theirs, got, w_gate, w_up, acc, (scale, hot_scale)
-    )
+    hidden, hot_hidden, *p3 = gate_up(
+        [dp ^ 1, dp ^ 2, dp ^ 3], hot, onehot, hot_onehot, rows, theirs, got, w_gate, w_up, acc, (scale, hot_scale),
+        (spread, hot_spread), w_down,
+    )
+
+    def whole_sum(own, *other):
+        return own.astype(F32) + jnp.concatenate(other, axis=0).astype(F32)
+
+    def swapped(found):
+        return [piece if i % 3 == 0 else swap(piece) for i, piece in enumerate(found)]
 
     def partial(group, hot):
-        own, other = down([dp ^ r for r in group], hot, spread, hot_spread, hidden, hot_hidden, w_down, part)
-        half = own.shape[0] // 2
-        found = []
-        for i in range(len(group)):
-            lanes = slice(i * part, (i + 1) * part)
-            theirs = [swap(other[:half, lanes]), swap(other[half:, lanes])]
-            found.append(own[:, lanes].astype(F32) + jnp.concatenate(theirs, axis=0).astype(F32))
-        return found
-
-    (p3,) = partial((3,), hot)
-    p3 = p3.astype(BF16)
+        return swapped(down([dp ^ r for r in group], hot, spread, hot_spread, hidden, hot_hidden, w_down, part))
+
+    far_rows = (lines - 1) * group_tok
+    p3 = whole_sum(*swapped(p3)).astype(BF16)
     hot, p3 = after(hot, p3)
     corner = across[3](p3)
-    p1, p2 = partial((1, 2), hot)
-    p1, p2 = p1.astype(BF16), p2.astype(BF16)
-    hot, p1, p2, corner = after(hot, p1, p2, corner)
-    by_x, by_y = across[1](p1), across[2](p2)
-    (p0,) = partial((0,), hot)
-    total = p0 + corner.astype(F32) + by_x.astype(F32) + by_y.astype(F32)
-    out = total[(lines - 1) * group_tok :]
-    for i, s in enumerate(order):
-        out = out + along[lines - s](total[i * group_tok : (i + 1) * group_tok].astype(BF16)).astype(F32)
+    p12 = partial((1, 2), hot)
+    p12[0], p12[3], corner = after(p12[0], p12[3], corner)
+    p1, p2 = whole_sum(*p12[:3]).astype(BF16), whole_sum(*p12[3:]).astype(BF16)
+    hot, p1, p2 = after(hot, p1, p2)
+    by_x, by_y = across[1](p1[:far_rows]), across[2](p2[:far_rows])
+    p0 = partial((0,), hot)
+    p0[0], by_x, by_y = after(p0[0], by_x, by_y)
+    end_x, end_y = across[1](p1[far_rows:]), across[2](p2[far_rows:])
+    p0 = whole_sum(*p0) + corner.astype(F32)
+    total = (p0[:far_rows] + by_x.astype(F32) + by_y.astype(F32)).astype(BF16)
+    found = [along[lines - s](total[i * group_tok : (i + 1) * group_tok]) for i, s in enumerate(order)]
+    out = p0[far_rows:] + end_x.astype(F32) + end_y.astype(F32)
+    for piece in found:
+        out = out + piece.astype(F32)
     return out.astype(BF16)[None]
 
 

time: 145 us -> 141 us (0.972); the launches traced: 147 us -> 141 us
  waiting for transfers between devices: 44 us -> 35.9 us
  starting transfers between devices: 32.1 us -> 36.1 us
  Pallas kernels: 60.2 us -> 58.7 us
    ppermute x30 -> x32, waiting for transfers between devices: 44 us -> 35.9 us  [mover(): return lambda x: lax.ppermute(x, AXES, pairs)]
    pallas_call x3 -> x2, Pallas kernels: 24.1 us -> 17.7 us  [down(): pl.pallas_call(functools.partial(down_kernel, nq), in_specs=[scalars()] *...]
    pallas_call x2, Pallas kernels: 29.4 us -> 34.3 us  [gate_up(): pl.pallas_call(functools.partial(gate_up_kernel, tuple((len(p) // 2 for p...]
    ppermute x30 -> x32, starting transfers between devices: 32.1 us -> 36.1 us  [mover(): return lambda x: lax.ppermute(x, AXES, pairs)]
    unnamed x48 -> x46, local copies, waits for them, and re-layouts: 5.29 us -> 4.32 us
  transfers between devices with their start and end apart: 30 -> 32, of which waited for: 19 -> 11; matrix products, arithmetic and copies ran while one was open for 3% -> 3% of each run, Pallas kernels for 22% -> 23%
where the time goes in v3:
time: 141 us
  Pallas kernels  58.7 us (42%)
  starting transfers between devices  36.1 us (26%)
  waiting for transfers between devices  35.9 us (25%)
  local copies, waits for them, and re-layouts  5.63 us (4%)
  other arithmetic  4.07 us (3%)
    ppermute x32, starting transfers between devices, mover(): return lambda x: lax.ppermute(x, AXES, pairs)  36.1 us
    ppermute x32, waiting for transfers between devices, mover(): return lambda x: lax.ppermute(x, AXES, pairs)  35.9 us
    pallas_call x2, Pallas kernels, gate_up(): pl.pallas_call(functools.partial(gate_up_kernel, tuple((len(p) // 2 for p...  34.3 us
    pallas_call x2, Pallas kernels, down(): pl.pallas_call(functools.partial(down_kernel, nq), in_specs=[scalars()] *...  17.7 us
    pallas_call x2, Pallas kernels, staged(): pl.pallas_call(functools.partial(staged_kernel, body, len(given), len(inp...  6.66 us
    unnamed x46, local copies, waits for them, and re-layouts  4.32 us
  transfers between devices with their start and end apart: 32, of which 11 were waited for; matrix products, arithmetic and copies ran while one was open for 3% of the time, Pallas kernels for 23%

profile of v3, /device:TPU:0, one launch (start us, length us, event | category | flops | bytes accessed | tf_op | source)
XLA Modules:
  0.0 140.7 jit_solution(935344310646044828)
XLA Ops:
  3.2 3.7 %collective-permute-start.3 = (bf16[88,1152]{1,0:T(8,128)(2,1)S(1)}, bf16[88,1152]{1,0:T(8,128)(2,1)S(1)}, u32[]{:S(2)}, u32[]{:S(2)}) collective-permute-start(bf16[88,1152]{1,0:T(8,128)(2,1)S(1)} %concatenate.15.refs_0_), channel_id=1, source_target_pairs={{0,4},{1,5},{2,6},{3,7},{4,0},{5,1},{6,2},{7,3},{8,12},{9,13},{10,... | collective-permute-start | bytes 608264 | tf_op jit(solution)/shard_map/ppermute | solution.py:548
  8.9 8.2 %collective-permute-done.3.refs_3_ = bf16[88,1152]{1,0:T(8,128)(2,1)S(1)} collective-permute-done((bf16[88,1152]{1,0:T(8,128)(2,1)S(1)}, bf16[88,1152]{1,0:T(8,128)(2,1)S(1)}, u32[]{:S(2)}, u32[]{:S(2)}) %collective-permute-start.3) | collective-permute-done | bytes 202784 | tf_op jit(solution)/shard_map/ppermute | solution.py:548
  17.2 5.3 %collective-permute-done.1.refs_1_ = bf16[88,1152]{1,0:T(8,128)(2,1)S(1)} collective-permute-done((bf16[88,1152]{1,0:T(8,128)(2,1)S(1)}, bf16[88,1152]{1,0:T(8,128)(2,1)S(1)}, u32[]{:S(2)}, u32[]{:S(2)}) %collective-permute-start.1) | collective-permute-done | bytes 202784 | tf_op jit(solution)/shard_map/ppermute | solution.py:548
  23.2 2.5 %pack.1 = (bf16[264,1024]{1,0:T(8,128)(2,1)}, bf16[88,1024]{1,0:T(8,128)(2,1)}, bf16[352,128]{1,0:T(8,128)(2,1)}) custom-call(bf16[88,1152]{1,0:T(8,128)(2,1)} %copy-done.6, bf16[88,1152]{1,0:T(8,128)(2,1)} %copy-done.14, bf16[88,1152]{1,0:T(8,128)(2,1)} %copy-done.13, bf16[88,1152]{1,0:T(8,128)(2,1)} %copy-done.12), custom_call_target="tpu_custom_call" | custom-call | bytes 1000000 | tf_op jit(solution)/shard_map/pack/pallas_call | solution.py:133
  25.7 1.6 %collective-permute-start.7 = (bf16[264,1024]{1,0:T(8,128)(2,1)}, bf16[264,1024]{1,0:T(8,128)(2,1)S(1)}, u32[]{:S(2)}, u32[]{:S(2)}) collective-permute-start(bf16[264,1024]{1,0:T(8,128)(2,1)} %get-tuple-element.62.rest_0_), channel_id=1, source_target_pairs={{0,16},{1,17},{2,18},{3,19},{4,20},{5,21},{6,22},{7,23},{8,24},{9,... | collective-permute-start | bytes 1622024 | tf_op jit(solution)/shard_map/ppermute | solution.py:548
  27.3 1.5 %collective-permute-start.6 = (bf16[264,1024]{1,0:T(8,128)(2,1)}, bf16[264,1024]{1,0:T(8,128)(2,1)S(1)}, u32[]{:S(2)}, u32[]{:S(2)}) collective-permute-start(bf16[264,1024]{1,0:T(8,128)(2,1)} %get-tuple-element.62.rest_0_), channel_id=1, source_target_pairs={{0,8},{1,9},{2,10},{3,11},{4,12},{5,13},{6,14},{7,15},{8,0},{9,1},... | collective-permute-start | bytes 1622024 | tf_op jit(solution)/shard_map/ppermute | solution.py:548
  28.8 2.7 %collective-permute-start.9 = (bf16[88,1024]{1,0:T(8,128)(2,1)S(1)}, bf16[88,1024]{1,0:T(8,128)(2,1)S(1)}, u32[]{:S(2)}, u32[]{:S(2)}) collective-permute-start(bf16[88,1024]{1,0:T(8,128)(2,1)S(1)} %get-tuple-element.67), channel_id=1, source_target_pairs={{0,6},{1,7},{2,0},{3,1},{4,2},{5,3},{6,4},{7,5},{8,14},{9,15},{10,... | collective-permute-start | bytes 540680 | tf_op jit(solution)/shard_map/ppermute | solution.py:548
  31.5 2.7 %collective-permute-start.8 = (bf16[88,1024]{1,0:T(8,128)(2,1)S(1)}, bf16[88,1024]{1,0:T(8,128)(2,1)S(1)}, u32[]{:S(2)}, u32[]{:S(2)}) collective-permute-start(bf16[88,1024]{1,0:T(8,128)(2,1)S(1)} %get-tuple-element.67), channel_id=1, source_target_pairs={{0,2},{1,3},{2,4},{3,5},{4,6},{5,7},{6,0},{7,1},{8,10},{9,11},{10,... | collective-permute-start | bytes 540680 | tf_op jit(solution)/shard_map/ppermute | solution.py:548
  34.7 4.2 %places.1 = (bf16[896,704]{1,0:T(8,128)(2,1)}, bf16[240,704]{1,0:T(8,128)(2,1)}, bf16[704,896]{1,0:T(8,128)(2,1)}, bf16[704,240]{1,0:T(8,128)(2,1)}, f32[8,112,1...) custom-call(s32[1]{0:T(128)} %bitcast.1.refs_0_, bf16[352,128]{1,0:T(8,128)(2,1)} %get-tuple-element.57.refs_1_, ...), custom_call_target="tpu_custom_call" | custom-call | bytes 15000000 | tf_op jit(solution)/shard_map/places/pallas_call | solution.py:133
  38.9 9.9 %gate_up.2 = (f32[8,112,768]{2,1,0:T(8,128)}, f32[240,768]{1,0:T(8,128)}) custom-call(s32[1]{0:T(128)} %bitcast.quarter, s32[1]{0:T(128)} %get-tuple-element.93.busy, bf16[8,4096,384]{2,1,0:T(8,128)(2,1)} %wg.3, bf16[8,4096,384]{2,1,0:T(8,128)(2,1)} %wu.3, bf16[88,4096]{1,0:T(8,128)(2,1)} %bitcast.22, bf16[88,4096]{1,0:T(8,128)(2,1)} %copy-done.5, ...), custom_call_target="tpu_custom_call" | custom-call | tf_op jit(solution)/shard_map/gate_up/pallas_call | solution.py:395
  53.5 24.5 %gate_up.3 = (bf16[8,112,384]{2,1,0:T(8,128)(2,1)}, bf16[240,384]{1,0:T(8,128)(2,1)}, bf16[352,1024]{1,0:T(8,128)(2,1)}, bf16[176,1024]{1,0:T(8,128)(2,1)}, bf16[176,1024]{1,0:T(8,128)(2,1)}) custom-call(s32[3]{0:T(128)} %pad_add_fusion.quarter, s32[1]{0:T(128)} %get-tuple-element.93.busy, bf16[8,4096,384]{2,1,0:T(8,128)(2,1)} %wg.3, ...), custom_call_target="tpu_custom_call" | custom-call | tf_op jit(solution)/shard_map/gate_up/pallas_call | solution.py:395
  78.6 1.4 collective-permute-done.16
  81.8 2.5 %collective-permute-start.18 = (bf16[352,1024]{1,0:T(8,128)(2,1)S(1)}, bf16[352,1024]{1,0:T(8,128)(2,1)S(1)}, u32[]{:S(2)}, u32[]{:S(2)}) collective-permute-start(bf16[352,1024]{1,0:T(8,128)(2,1)S(1)} %add_convert_fusion.2), channel_id=1, source_target_pairs={{0,24},{1,25},{2,26},{3,27},{4,28},{5,29},{6,30},{7,31},{8,16},{9,... | collective-permute-start | bytes 2162696 | tf_op jit(solution)/shard_map/ppermute | solution.py:548
  85.5 11.2 %down.2 = (bf16[352,1024]{1,0:T(8,128)(2,1)S(1)}, bf16[176,1024]{1,0:T(8,128)(2,1)S(1)}, bf16[176,1024]{1,0:T(8,128)(2,1)S(1)}, bf16[352,1024]{1,0:T(8,128)(2,1)...) custom-call(s32[2]{0:T(128)S(1)} %pad_add_fusion.1.quarter, s32[1]{0:T(128)} %get-tuple-element.93.busy, ...), custom_call_target="tpu_custom_call" | custom-call | tf_op jit(solution)/shard_map/down/pallas_call | solution.py:517
  97.8 3.2 %collective-permute-done.18 = bf16[352,1024]{1,0:T(8,128)(2,1)S(1)} collective-permute-done((bf16[352,1024]{1,0:T(8,128)(2,1)S(1)}, bf16[352,1024]{1,0:T(8,128)(2,1)S(1)}, u32[]{:S(2)}, u32[]{:S(2)}) %collective-permute-start.18) | collective-permute-done | bytes 720928 | tf_op jit(solution)/shard_map/ppermute | solution.py:548
  101.6 1.6 %collective-permute-start.24 = (bf16[264,1024]{1,0:T(8,128)(2,1)S(1)}, bf16[264,1024]{1,0:T(8,128)(2,1)S(1)}, u32[]{:S(2)}, u32[]{:S(2)}) collective-permute-start(bf16[264,1024]{1,0:T(8,128)(2,1)S(1)} %slice.28), channel_id=1, source_target_pairs={{0,16},{1,17},{2,18},{3,19},{4,20},{5,21},{6,22},{7,23},{8,24},{9,... | collective-permute-start | bytes 1622024 | tf_op jit(solution)/shard_map/ppermute | solution.py:548
  103.2 1.6 %collective-permute-start.23 = (bf16[264,1024]{1,0:T(8,128)(2,1)S(1)}, bf16[264,1024]{1,0:T(8,128)(2,1)S(1)}, u32[]{:S(2)}, u32[]{:S(2)}) collective-permute-start(bf16[264,1024]{1,0:T(8,128)(2,1)S(1)} %slice.27), channel_id=1, source_target_pairs={{0,8},{1,9},{2,10},{3,11},{4,12},{5,13},{6,14},{7,15},{8,0},{9,1},... | collective-permute-start | bytes 1622024 | tf_op jit(solution)/shard_map/ppermute | solution.py:548
  104.8 6.5 %down.3 = (bf16[352,1024]{1,0:T(8,128)(2,1)S(1)}, bf16[176,1024]{1,0:T(8,128)(2,1)S(1)}, bf16[176,1024]{1,0:T(8,128)(2,1)S(1)}) custom-call(s32[1]{0:T(128)} %bitcast.quarter, s32[1]{0:T(128)} %get-tuple-element.93.busy, bf16[704,896]{1,0:T(8,128)(2,1)S(1)} %copy-done, bf16[704,240]{1,0:T(8,128)(2,1)S(1)} %copy-done.1, bf16[8,112,384]{2,1,0:T(8,128)(2,1)S(1)} %copy-done.3, ...), custom_call_target="tpu_custom_call" | custom-call | tf_op jit(solution)/shard_map/down/pallas_call | solution.py:517
  112.5 3.2 %collective-permute-done.24 = bf16[264,1024]{1,0:T(8,128)(2,1)S(1)} collective-permute-done((bf16[264,1024]{1,0:T(8,128)(2,1)S(1)}, bf16[264,1024]{1,0:T(8,128)(2,1)S(1)}, u32[]{:S(2)}, u32[]{:S(2)}) %collective-permute-start.24) | collective-permute-done | bytes 540704 | tf_op jit(solution)/shard_map/ppermute | solution.py:548
  115.7 2.4 %collective-permute-start.27 = (bf16[88,1024]{1,0:T(8,128)(2,1)S(1)}, bf16[88,1024]{1,0:T(8,128)(2,1)S(1)}, u32[]{:S(2)}, u32[]{:S(2)}) collective-permute-start(bf16[88,1024]{1,0:T(8,128)(2,1)S(1)} %slice.30), channel_id=1, source_target_pairs={{0,8},{1,9},{2,10},{3,11},{4,12},{5,13},{6,14},{7,15},{8,0},{9,1},... | collective-permute-start | bytes 540680 | tf_op jit(solution)/shard_map/ppermute | solution.py:548
  118.8 2.0 %collective-permute-start.29 = (bf16[88,1024]{1,0:T(8,128)(2,1)S(1)}, bf16[88,1024]{1,0:T(8,128)(2,1)S(1)}, u32[]{:S(2)}, u32[]{:S(2)}) collective-permute-start(bf16[88,1024]{1,0:T(8,128)(2,1)S(1)} %get-tuple-element.105), channel_id=1, source_target_pairs={{0,6},{1,7},{2,0},{3,1},{4,2},{5,3},{6,4},{7,5},{8,14},{9,15},{10,... | collective-permute-start | bytes 540680 | tf_op jit(solution)/shard_map/ppermute | solution.py:548
  120.8 5.0 %collective-permute-start.31 = (bf16[88,1024]{1,0:T(8,128)(2,1)S(1)}, bf16[88,1024]{1,0:T(8,128)(2,1)S(1)}, u32[]{:S(2)}, u32[]{:S(2)}) collective-permute-start(bf16[88,1024]{1,0:T(8,128)(2,1)S(1)} %get-tuple-element.106), channel_id=1, source_target_pairs={{0,4},{1,5},{2,6},{3,7},{4,0},{5,1},{6,2},{7,3},{8,12},{9,13},{10,... | collective-permute-start | bytes 540680 | tf_op jit(solution)/shard_map/ppermute | solution.py:548
  125.7 1.9 %collective-permute-start.30 = (bf16[88,1024]{1,0:T(8,128)(2,1)S(1)}, bf16[88,1024]{1,0:T(8,128)(2,1)S(1)}, u32[]{:S(2)}, u32[]{:S(2)}) collective-permute-start(bf16[88,1024]{1,0:T(8,128)(2,1)S(1)} %get-tuple-element.107), channel_id=1, source_target_pairs={{0,2},{1,3},{2,4},{3,5},{4,6},{5,7},{6,0},{7,1},{8,10},{9,11},{10,... | collective-permute-start | bytes 540680 | tf_op jit(solution)/shard_map/ppermute | solution.py:548
  127.7 12.2 %collective-permute-done.31 = bf16[88,1024]{1,0:T(8,128)(2,1)S(1)} collective-permute-done((bf16[88,1024]{1,0:T(8,128)(2,1)S(1)}, bf16[88,1024]{1,0:T(8,128)(2,1)S(1)}, u32[]{:S(2)}, u32[]{:S(2)}) %collective-permute-start.31) | collective-permute-done | bytes 180256 | tf_op jit(solution)/shard_map/ppermute | solution.py:548
  (110 shorter events, 19.1 us)
Async XLA Ops:
  0.0 22.5 %collective-permute-start = (bf16[88,4096]{1,0:T(8,128)(2,1)}, bf16[88,4096]{1,0:T(8,128)(2,1)S(1)}, u32[]{:S(2)}, u32[]{:S(2)}) collective-permute-start(bf16[88,4096]{1,0:T(8,128)(2,1)} %bitcast.21), channel_id=1, source_target_pairs={{0,1},{1,0},{2,3},{3,2},{4,5},{5,4},{6,7},{7,6},{8,9},{9,8},{10,11... | collective-permute-start | bytes 2162696 | tf_op jit(solution)/shard_map/ppermute | solution.py:548
  3.2 13.9 %collective-permute-start.3 = (bf16[88,1152]{1,0:T(8,128)(2,1)S(1)}, bf16[88,1152]{1,0:T(8,128)(2,1)S(1)}, u32[]{:S(2)}, u32[]{:S(2)}) collective-permute-start(bf16[88,1152]{1,0:T(8,128)(2,1)S(1)} %concatenate.15.refs_0_), channel_id=1, source_target_pairs={{0,4},{1,5},{2,6},{3,7},{4,0},{5,1},{6,2},{7,3},{8,12},{9,13},{10,... | collective-permute-start | bytes 608264 | tf_op jit(solution)/shard_map/ppermute | solution.py:548
  6.9 10.3 %collective-permute-start.2 = (bf16[88,1152]{1,0:T(8,128)(2,1)S(1)}, bf16[88,1152]{1,0:T(8,128)(2,1)S(1)}, u32[]{:S(2)}, u32[]{:S(2)}) collective-permute-start(bf16[88,1152]{1,0:T(8,128)(2,1)S(1)} %concatenate.15.refs_0_), channel_id=1, source_target_pairs={{0,6},{1,7},{2,0},{3,1},{4,2},{5,3},{6,4},{7,5},{8,14},{9,15},{10,... | collective-permute-start | bytes 608264 | tf_op jit(solution)/shard_map/ppermute | solution.py:548
  8.2 14.3 %collective-permute-start.1 = (bf16[88,1152]{1,0:T(8,128)(2,1)S(1)}, bf16[88,1152]{1,0:T(8,128)(2,1)S(1)}, u32[]{:S(2)}, u32[]{:S(2)}) collective-permute-start(bf16[88,1152]{1,0:T(8,128)(2,1)S(1)} %concatenate.15.refs_0_), channel_id=1, source_target_pairs={{0,2},{1,3},{2,4},{3,5},{4,6},{5,7},{6,0},{7,1},{8,10},{9,11},{10,... | collective-permute-start | bytes 608264 | tf_op jit(solution)/shard_map/ppermute | solution.py:548
  25.6 8.6 %collective-permute-start.5 = (bf16[264,1024]{1,0:T(8,128)(2,1)}, bf16[264,1024]{1,0:T(8,128)(2,1)S(1)}, u32[]{:S(2)}, u32[]{:S(2)}) collective-permute-start(bf16[264,1024]{1,0:T(8,128)(2,1)} %get-tuple-element.62.rest_0_), channel_id=1, source_target_pairs={{0,1},{1,0},{2,3},{3,2},{4,5},{5,4},{6,7},{7,6},{8,9},{9,8},{10,11... | collective-permute-start | bytes 1622024 | tf_op jit(solution)/shard_map/ppermute | solution.py:548
  25.7 23.2 %collective-permute-start.7 = (bf16[264,1024]{1,0:T(8,128)(2,1)}, bf16[264,1024]{1,0:T(8,128)(2,1)S(1)}, u32[]{:S(2)}, u32[]{:S(2)}) collective-permute-start(bf16[264,1024]{1,0:T(8,128)(2,1)} %get-tuple-element.62.rest_0_), channel_id=1, source_target_pairs={{0,16},{1,17},{2,18},{3,19},{4,20},{5,21},{6,22},{7,23},{8,24},{9,... | collective-permute-start | bytes 1622024 | tf_op jit(solution)/shard_map/ppermute | solution.py:548
  27.3 21.6 %collective-permute-start.6 = (bf16[264,1024]{1,0:T(8,128)(2,1)}, bf16[264,1024]{1,0:T(8,128)(2,1)S(1)}, u32[]{:S(2)}, u32[]{:S(2)}) collective-permute-start(bf16[264,1024]{1,0:T(8,128)(2,1)} %get-tuple-element.62.rest_0_), channel_id=1, source_target_pairs={{0,8},{1,9},{2,10},{3,11},{4,12},{5,13},{6,14},{7,15},{8,0},{9,1},... | collective-permute-start | bytes 1622024 | tf_op jit(solution)/shard_map/ppermute | solution.py:548
  28.8 20.0 %collective-permute-start.9 = (bf16[88,1024]{1,0:T(8,128)(2,1)S(1)}, bf16[88,1024]{1,0:T(8,128)(2,1)S(1)}, u32[]{:S(2)}, u32[]{:S(2)}) collective-permute-start(bf16[88,1024]{1,0:T(8,128)(2,1)S(1)} %get-tuple-element.67), channel_id=1, source_target_pairs={{0,6},{1,7},{2,0},{3,1},{4,2},{5,3},{6,4},{7,5},{8,14},{9,15},{10,... | collective-permute-start | bytes 540680 | tf_op jit(solution)/shard_map/ppermute | solution.py:548
  31.5 17.3 %collective-permute-start.8 = (bf16[88,1024]{1,0:T(8,128)(2,1)S(1)}, bf16[88,1024]{1,0:T(8,128)(2,1)S(1)}, u32[]{:S(2)}, u32[]{:S(2)}) collective-permute-start(bf16[88,1024]{1,0:T(8,128)(2,1)S(1)} %get-tuple-element.67), channel_id=1, source_target_pairs={{0,2},{1,3},{2,4},{3,5},{4,6},{5,7},{6,0},{7,1},{8,10},{9,11},{10,... | collective-permute-start | bytes 540680 | tf_op jit(solution)/shard_map/ppermute | solution.py:548
  34.2 14.6 %collective-permute-start.10 = (bf16[88,1024]{1,0:T(8,128)(2,1)}, bf16[88,1024]{1,0:T(8,128)(2,1)S(1)}, u32[]{:S(2)}, u32[]{:S(2)}) collective-permute-start(bf16[88,1024]{1,0:T(8,128)(2,1)} %get-tuple-element.68), channel_id=1, source_target_pairs={{0,24},{1,25},{2,26},{3,27},{4,28},{5,29},{6,30},{7,31},{8,16},{9,... | collective-permute-start | bytes 540680 | tf_op jit(solution)/shard_map/ppermute | solution.py:548
  81.8 19.1 %collective-permute-start.18 = (bf16[352,1024]{1,0:T(8,128)(2,1)S(1)}, bf16[352,1024]{1,0:T(8,128)(2,1)S(1)}, u32[]{:S(2)}, u32[]{:S(2)}) collective-permute-start(bf16[352,1024]{1,0:T(8,128)(2,1)S(1)} %add_convert_fusion.2), channel_id=1, source_target_pairs={{0,24},{1,25},{2,26},{3,27},{4,28},{5,29},{6,30},{7,31},{8,16},{9,... | collective-permute-start | bytes 2162696 | tf_op jit(solution)/shard_map/ppermute | solution.py:548
  96.7 4.2 %collective-permute-start.19 = (bf16[176,1024]{1,0:T(8,128)(2,1)S(1)}, bf16[176,1024]{1,0:T(8,128)(2,1)S(1)}, u32[]{:S(2)}, u32[]{:S(2)}) collective-permute-start(bf16[176,1024]{1,0:T(8,128)(2,1)S(1)} %get-tuple-element.88), channel_id=1, source_target_pairs={{0,1},{1,0},{2,3},{3,2},{4,5},{5,4},{6,7},{7,6},{8,9},{9,8},{10,11... | collective-permute-start | bytes 1081352 | tf_op jit(solution)/shard_map/ppermute | solution.py:548
  96.8 4.2 %collective-permute-start.20 = (bf16[176,1024]{1,0:T(8,128)(2,1)S(1)}, bf16[176,1024]{1,0:T(8,128)(2,1)S(1)}, u32[]{:S(2)}, u32[]{:S(2)}) collective-permute-start(bf16[176,1024]{1,0:T(8,128)(2,1)S(1)} %get-tuple-element.89), channel_id=1, source_target_pairs={{0,1},{1,0},{2,3},{3,2},{4,5},{5,4},{6,7},{7,6},{8,9},{9,8},{10,11... | collective-permute-start | bytes 1081352 | tf_op jit(solution)/shard_map/ppermute | solution.py:548
  97.3 3.9 %collective-permute-start.21 = (bf16[176,1024]{1,0:T(8,128)(2,1)S(1)}, bf16[176,1024]{1,0:T(8,128)(2,1)S(1)}, u32[]{:S(2)}, u32[]{:S(2)}) collective-permute-start(bf16[176,1024]{1,0:T(8,128)(2,1)S(1)} %get-tuple-element.91), channel_id=1, source_target_pairs={{0,1},{1,0},{2,3},{3,2},{4,5},{5,4},{6,7},{7,6},{8,9},{9,8},{10,11... | collective-permute-start | bytes 1081352 | tf_op jit(solution)/shard_map/ppermute | solution.py:548
  97.4 3.9 %collective-permute-start.22 = (bf16[176,1024]{1,0:T(8,128)(2,1)S(1)}, bf16[176,1024]{1,0:T(8,128)(2,1)S(1)}, u32[]{:S(2)}, u32[]{:S(2)}) collective-permute-start(bf16[176,1024]{1,0:T(8,128)(2,1)S(1)} %get-tuple-element.92), channel_id=1, source_target_pairs={{0,1},{1,0},{2,3},{3,2},{4,5},{5,4},{6,7},{7,6},{8,9},{9,8},{10,11... | collective-permute-start | bytes 1081352 | tf_op jit(solution)/shard_map/ppermute | solution.py:548
  101.6 14.1 %collective-permute-start.24 = (bf16[264,1024]{1,0:T(8,128)(2,1)S(1)}, bf16[264,1024]{1,0:T(8,128)(2,1)S(1)}, u32[]{:S(2)}, u32[]{:S(2)}) collective-permute-start(bf16[264,1024]{1,0:T(8,128)(2,1)S(1)} %slice.28), channel_id=1, source_target_pairs={{0,16},{1,17},{2,18},{3,19},{4,20},{5,21},{6,22},{7,23},{8,24},{9,... | collective-permute-start | bytes 1622024 | tf_op jit(solution)/shard_map/ppermute | solution.py:548
  103.2 14.8 %collective-permute-start.23 = (bf16[264,1024]{1,0:T(8,128)(2,1)S(1)}, bf16[264,1024]{1,0:T(8,128)(2,1)S(1)}, u32[]{:S(2)}, u32[]{:S(2)}) collective-permute-start(bf16[264,1024]{1,0:T(8,128)(2,1)S(1)} %slice.27), channel_id=1, source_target_pairs={{0,8},{1,9},{2,10},{3,11},{4,12},{5,13},{6,14},{7,15},{8,0},{9,1},... | collective-permute-start | bytes 1622024 | tf_op jit(solution)/shard_map/ppermute | solution.py:548
  111.3 6.8 %collective-permute-start.25 = (bf16[176,1024]{1,0:T(8,128)(2,1)S(1)}, bf16[176,1024]{1,0:T(8,128)(2,1)S(1)}, u32[]{:S(2)}, u32[]{:S(2)}) collective-permute-start(bf16[176,1024]{1,0:T(8,128)(2,1)S(1)} %get-tuple-element.98), channel_id=1, source_target_pairs={{0,1},{1,0},{2,3},{3,2},{4,5},{5,4},{6,7},{7,6},{8,9},{9,8},{10,11... | collective-permute-start | bytes 1081352 | tf_op jit(solution)/shard_map/ppermute | solution.py:548
  111.3 6.7 %collective-permute-start.26 = (bf16[176,1024]{1,0:T(8,128)(2,1)S(1)}, bf16[176,1024]{1,0:T(8,128)(2,1)S(1)}, u32[]{:S(2)}, u32[]{:S(2)}) collective-permute-start(bf16[176,1024]{1,0:T(8,128)(2,1)S(1)} %get-tuple-element.99), channel_id=1, source_target_pairs={{0,1},{1,0},{2,3},{3,2},{4,5},{5,4},{6,7},{7,6},{8,9},{9,8},{10,11... | collective-permute-start | bytes 1081352 | tf_op jit(solution)/shard_map/ppermute | solution.py:548
  111.9 15.8 %collective-permute-start.28 = (bf16[88,1024]{1,0:T(8,128)(2,1)S(1)}, bf16[88,1024]{1,0:T(8,128)(2,1)S(1)}, u32[]{:S(2)}, u32[]{:S(2)}) collective-permute-start(bf16[88,1024]{1,0:T(8,128)(2,1)S(1)} %slice.31), channel_id=1, source_target_pairs={{0,16},{1,17},{2,18},{3,19},{4,20},{5,21},{6,22},{7,23},{8,24},{9,... | collective-permute-start | bytes 540680 | tf_op jit(solution)/shard_map/ppermute | solution.py:548
  115.7 12.0 %collective-permute-start.27 = (bf16[88,1024]{1,0:T(8,128)(2,1)S(1)}, bf16[88,1024]{1,0:T(8,128)(2,1)S(1)}, u32[]{:S(2)}, u32[]{:S(2)}) collective-permute-start(bf16[88,1024]{1,0:T(8,128)(2,1)S(1)} %slice.30), channel_id=1, source_target_pairs={{0,8},{1,9},{2,10},{3,11},{4,12},{5,13},{6,14},{7,15},{8,0},{9,1},... | collective-permute-start | bytes 540680 | tf_op jit(solution)/shard_map/ppermute | solution.py:548
  118.8 8.9 %collective-permute-start.29 = (bf16[88,1024]{1,0:T(8,128)(2,1)S(1)}, bf16[88,1024]{1,0:T(8,128)(2,1)S(1)}, u32[]{:S(2)}, u32[]{:S(2)}) collective-permute-start(bf16[88,1024]{1,0:T(8,128)(2,1)S(1)} %get-tuple-element.105), channel_id=1, source_target_pairs={{0,6},{1,7},{2,0},{3,1},{4,2},{5,3},{6,4},{7,5},{8,14},{9,15},{10,... | collective-permute-start | bytes 540680 | tf_op jit(solution)/shard_map/ppermute | solution.py:548
  120.8 19.1 %collective-permute-start.31 = (bf16[88,1024]{1,0:T(8,128)(2,1)S(1)}, bf16[88,1024]{1,0:T(8,128)(2,1)S(1)}, u32[]{:S(2)}, u32[]{:S(2)}) collective-permute-start(bf16[88,1024]{1,0:T(8,128)(2,1)S(1)} %get-tuple-element.106), channel_id=1, source_target_pairs={{0,4},{1,5},{2,6},{3,7},{4,0},{5,1},{6,2},{7,3},{8,12},{9,13},{10,... | collective-permute-start | bytes 540680 | tf_op jit(solution)/shard_map/ppermute | solution.py:548
  125.7 14.2 %collective-permute-start.30 = (bf16[88,1024]{1,0:T(8,128)(2,1)S(1)}, bf16[88,1024]{1,0:T(8,128)(2,1)S(1)}, u32[]{:S(2)}, u32[]{:S(2)}) collective-permute-start(bf16[88,1024]{1,0:T(8,128)(2,1)S(1)} %get-tuple-element.107), channel_id=1, source_target_pairs={{0,2},{1,3},{2,4},{3,5},{4,6},{5,7},{6,0},{7,1},{8,10},{9,11},{10,... | collective-permute-start | bytes 540680 | tf_op jit(solution)/shard_map/ppermute | solution.py:548
  (30 other events, 121.5 us)

commit v4 on v3

--- a/solution.py
+++ b/solution.py
@@ -273,9 +273,9 @@
         for copy in copies:
             copy.start()
 
-    start(loads[:2] + pieces[0] + copies(0, 0))
-    ahead = [copies(e, e) for e in range(1, min(depth, n))]
-    ahead = [sum(pieces[1:], [])] + ahead[:1] + [loads[2:]] + ahead[1:]
+    start(loads[:2] + sum(pieces, []))
+    ahead = [copies(e, e) for e in range(min(depth, n))]
+    ahead = ahead[:2] + [loads[2:]] + ahead[2:]
     for i in range(nq):
         lanes = slice(i * part, (i + 1) * part)
         for copy in (loads[:2] if i == 0 else []) + pieces[i]:
@@ -577,7 +577,7 @@
     theirs = swap(rows)
     got = after(theirs, *[along[s](first) for s in order])
     theirs, got = got[0], got[1:]
-    corner = after(mine[1], *got)[0]
+    corner = after(mine[1], got[-1])[0]
     near, tail, table = pack(first, got, part)
     corner = [along[s](corner) for s in order[:2]] + [across[3](tail)]
     by_x, by_y = across[1](near), across[2](near)

time: 141 us -> 139 us (0.986)
  starting transfers between devices: 36.1 us -> 33.5 us
    ppermute x32, starting transfers between devices: 36.1 us -> 33.5 us  [mover(): return lambda x: lax.ppermute(x, AXES, pairs)]
  transfers between devices with their start and end apart: 32 -> 32, of which waited for: 11 -> 12; matrix products, arithmetic and copies ran while one was open for 3% -> 3% of each run, Pallas kernels for 23% -> 23%
where the time goes in v4:
time: 139 us; the launch traced here: 138 us
  Pallas kernels  58.5 us (42%)
  waiting for transfers between devices  36.2 us (26%)
  starting transfers between devices  33.5 us (24%)
  local copies, waits for them, and re-layouts  5.63 us (4%)
  other arithmetic  4.07 us (3%)
    ppermute x32, waiting for transfers between devices, mover(): return lambda x: lax.ppermute(x, AXES, pairs)  36.2 us
    pallas_call x2, Pallas kernels, gate_up(): pl.pallas_call(functools.partial(gate_up_kernel, tuple((len(p) // 2 for p...  34.2 us
    ppermute x32, starting transfers between devices, mover(): return lambda x: lax.ppermute(x, AXES, pairs)  33.5 us
    pallas_call x2, Pallas kernels, down(): pl.pallas_call(functools.partial(down_kernel, nq), in_specs=[scalars()] *...  17.7 us
    pallas_call x2, Pallas kernels, staged(): pl.pallas_call(functools.partial(staged_kernel, body, len(given), len(inp...  6.66 us
    unnamed x46, local copies, waits for them, and re-layouts  4.32 us
  transfers between devices with their start and end apart: 32, of which 12 were waited for; matrix products, arithmetic and copies ran while one was open for 3% of the time, Pallas kernels for 23%

profile of v4, /device:TPU:0, one launch (start us, length us, event | category | flops | bytes accessed | tf_op | source)
XLA Modules:
  0.0 138.4 jit_solution(3223633185150071015)
XLA Ops:
  3.2 3.7 %collective-permute-start.3 = (bf16[88,1152]{1,0:T(8,128)(2,1)S(1)}, bf16[88,1152]{1,0:T(8,128)(2,1)S(1)}, u32[]{:S(2)}, u32[]{:S(2)}) collective-permute-start(bf16[88,1152]{1,0:T(8,128)(2,1)S(1)} %concatenate.15.refs_0_), channel_id=1, source_target_pairs={{0,4},{1,5},{2,6},{3,7},{4,0},{5,1},{6,2},{7,3},{8,12},{9,13},{10,... | collective-permute-start | bytes 608264 | tf_op jit(solution)/shard_map/ppermute | solution.py:548
  8.9 8.2 %collective-permute-done.3.refs_3_ = bf16[88,1152]{1,0:T(8,128)(2,1)S(1)} collective-permute-done((bf16[88,1152]{1,0:T(8,128)(2,1)S(1)}, bf16[88,1152]{1,0:T(8,128)(2,1)S(1)}, u32[]{:S(2)}, u32[]{:S(2)}) %collective-permute-start.3) | collective-permute-done | bytes 202784 | tf_op jit(solution)/shard_map/ppermute | solution.py:548
  17.2 5.3 %collective-permute-done.1.refs_1_ = bf16[88,1152]{1,0:T(8,128)(2,1)S(1)} collective-permute-done((bf16[88,1152]{1,0:T(8,128)(2,1)S(1)}, bf16[88,1152]{1,0:T(8,128)(2,1)S(1)}, u32[]{:S(2)}, u32[]{:S(2)}) %collective-permute-start.1) | collective-permute-done | bytes 202784 | tf_op jit(solution)/shard_map/ppermute | solution.py:548
  23.2 2.5 %pack.1 = (bf16[264,1024]{1,0:T(8,128)(2,1)}, bf16[88,1024]{1,0:T(8,128)(2,1)}, bf16[352,128]{1,0:T(8,128)(2,1)}) custom-call(bf16[88,1152]{1,0:T(8,128)(2,1)} %copy-done.6, bf16[88,1152]{1,0:T(8,128)(2,1)} %copy-done.14, bf16[88,1152]{1,0:T(8,128)(2,1)} %copy-done.13, bf16[88,1152]{1,0:T(8,128)(2,1)} %copy-done.12), custom_call_target="tpu_custom_call" | custom-call | bytes 1000000 | tf_op jit(solution)/shard_map/pack/pallas_call | solution.py:133
  25.7 1.6 %collective-permute-start.7 = (bf16[264,1024]{1,0:T(8,128)(2,1)}, bf16[264,1024]{1,0:T(8,128)(2,1)S(1)}, u32[]{:S(2)}, u32[]{:S(2)}) collective-permute-start(bf16[264,1024]{1,0:T(8,128)(2,1)} %get-tuple-element.62.rest_0_), channel_id=1, source_target_pairs={{0,16},{1,17},{2,18},{3,19},{4,20},{5,21},{6,22},{7,23},{8,24},{9,... | collective-permute-start | bytes 1622024 | tf_op jit(solution)/shard_map/ppermute | solution.py:548
  27.3 1.5 %collective-permute-start.6 = (bf16[264,1024]{1,0:T(8,128)(2,1)}, bf16[264,1024]{1,0:T(8,128)(2,1)S(1)}, u32[]{:S(2)}, u32[]{:S(2)}) collective-permute-start(bf16[264,1024]{1,0:T(8,128)(2,1)} %get-tuple-element.62.rest_0_), channel_id=1, source_target_pairs={{0,8},{1,9},{2,10},{3,11},{4,12},{5,13},{6,14},{7,15},{8,0},{9,1},... | collective-permute-start | bytes 1622024 | tf_op jit(solution)/shard_map/ppermute | solution.py:548
  28.8 2.7 %collective-permute-start.9 = (bf16[88,1024]{1,0:T(8,128)(2,1)S(1)}, bf16[88,1024]{1,0:T(8,128)(2,1)S(1)}, u32[]{:S(2)}, u32[]{:S(2)}) collective-permute-start(bf16[88,1024]{1,0:T(8,128)(2,1)S(1)} %get-tuple-element.67), channel_id=1, source_target_pairs={{0,6},{1,7},{2,0},{3,1},{4,2},{5,3},{6,4},{7,5},{8,14},{9,15},{10,... | collective-permute-start | bytes 540680 | tf_op jit(solution)/shard_map/ppermute | solution.py:548
  31.5 2.7 %collective-permute-start.8 = (bf16[88,1024]{1,0:T(8,128)(2,1)S(1)}, bf16[88,1024]{1,0:T(8,128)(2,1)S(1)}, u32[]{:S(2)}, u32[]{:S(2)}) collective-permute-start(bf16[88,1024]{1,0:T(8,128)(2,1)S(1)} %get-tuple-element.67), channel_id=1, source_target_pairs={{0,2},{1,3},{2,4},{3,5},{4,6},{5,7},{6,0},{7,1},{8,10},{9,11},{10,... | collective-permute-start | bytes 540680 | tf_op jit(solution)/shard_map/ppermute | solution.py:548
  34.7 4.2 %places.1 = (bf16[896,704]{1,0:T(8,128)(2,1)}, bf16[240,704]{1,0:T(8,128)(2,1)}, bf16[704,896]{1,0:T(8,128)(2,1)}, bf16[704,240]{1,0:T(8,128)(2,1)}, f32[8,112,1...) custom-call(s32[1]{0:T(128)} %bitcast.1.refs_0_, bf16[352,128]{1,0:T(8,128)(2,1)} %get-tuple-element.57.refs_1_, ...), custom_call_target="tpu_custom_call" | custom-call | bytes 15000000 | tf_op jit(solution)/shard_map/places/pallas_call | solution.py:133
  38.9 9.6 %gate_up.2 = (f32[8,112,768]{2,1,0:T(8,128)}, f32[240,768]{1,0:T(8,128)}) custom-call(s32[1]{0:T(128)} %bitcast.quarter, s32[1]{0:T(128)} %get-tuple-element.93.busy, bf16[8,4096,384]{2,1,0:T(8,128)(2,1)} %wg.3, bf16[8,4096,384]{2,1,0:T(8,128)(2,1)} %wu.3, bf16[88,4096]{1,0:T(8,128)(2,1)} %bitcast.22, bf16[88,4096]{1,0:T(8,128)(2,1)} %copy-done.5, ...), custom_call_target="tpu_custom_call" | custom-call | tf_op jit(solution)/shard_map/gate_up/pallas_call | solution.py:395
  53.3 24.6 %gate_up.3 = (bf16[8,112,384]{2,1,0:T(8,128)(2,1)}, bf16[240,384]{1,0:T(8,128)(2,1)}, bf16[352,1024]{1,0:T(8,128)(2,1)}, bf16[176,1024]{1,0:T(8,128)(2,1)}, bf16[176,1024]{1,0:T(8,128)(2,1)}) custom-call(s32[3]{0:T(128)} %pad_add_fusion.quarter, s32[1]{0:T(128)} %get-tuple-element.93.busy, bf16[8,4096,384]{2,1,0:T(8,128)(2,1)} %wg.3, ...), custom_call_target="tpu_custom_call" | custom-call | tf_op jit(solution)/shard_map/gate_up/pallas_call | solution.py:395
  78.5 1.4 collective-permute-done.16
  80.3 1.4 add_convert_fusion.2
  81.7 2.5 %collective-permute-start.18 = (bf16[352,1024]{1,0:T(8,128)(2,1)S(1)}, bf16[352,1024]{1,0:T(8,128)(2,1)S(1)}, u32[]{:S(2)}, u32[]{:S(2)}) collective-permute-start(bf16[352,1024]{1,0:T(8,128)(2,1)S(1)} %add_convert_fusion.2), channel_id=1, source_target_pairs={{0,24},{1,25},{2,26},{3,27},{4,28},{5,29},{6,30},{7,31},{8,16},{9,... | collective-permute-start | bytes 2162696 | tf_op jit(solution)/shard_map/ppermute | solution.py:548
  85.4 11.2 %down.2 = (bf16[352,1024]{1,0:T(8,128)(2,1)S(1)}, bf16[176,1024]{1,0:T(8,128)(2,1)S(1)}, bf16[176,1024]{1,0:T(8,128)(2,1)S(1)}, bf16[352,1024]{1,0:T(8,128)(2,1)...) custom-call(s32[2]{0:T(128)S(1)} %pad_add_fusion.1.quarter, s32[1]{0:T(128)} %get-tuple-element.93.busy, ...), custom_call_target="tpu_custom_call" | custom-call | tf_op jit(solution)/shard_map/down/pallas_call | solution.py:517
  97.7 3.2 %collective-permute-done.18 = bf16[352,1024]{1,0:T(8,128)(2,1)S(1)} collective-permute-done((bf16[352,1024]{1,0:T(8,128)(2,1)S(1)}, bf16[352,1024]{1,0:T(8,128)(2,1)S(1)}, u32[]{:S(2)}, u32[]{:S(2)}) %collective-permute-start.18) | collective-permute-done | bytes 720928 | tf_op jit(solution)/shard_map/ppermute | solution.py:548
  101.5 1.6 %collective-permute-start.24 = (bf16[264,1024]{1,0:T(8,128)(2,1)S(1)}, bf16[264,1024]{1,0:T(8,128)(2,1)S(1)}, u32[]{:S(2)}, u32[]{:S(2)}) collective-permute-start(bf16[264,1024]{1,0:T(8,128)(2,1)S(1)} %slice.28), channel_id=1, source_target_pairs={{0,16},{1,17},{2,18},{3,19},{4,20},{5,21},{6,22},{7,23},{8,24},{9,... | collective-permute-start | bytes 1622024 | tf_op jit(solution)/shard_map/ppermute | solution.py:548
  103.1 1.6 %collective-permute-start.23 = (bf16[264,1024]{1,0:T(8,128)(2,1)S(1)}, bf16[264,1024]{1,0:T(8,128)(2,1)S(1)}, u32[]{:S(2)}, u32[]{:S(2)}) collective-permute-start(bf16[264,1024]{1,0:T(8,128)(2,1)S(1)} %slice.27), channel_id=1, source_target_pairs={{0,8},{1,9},{2,10},{3,11},{4,12},{5,13},{6,14},{7,15},{8,0},{9,1},... | collective-permute-start | bytes 1622024 | tf_op jit(solution)/shard_map/ppermute | solution.py:548
  104.7 6.5 %down.3 = (bf16[352,1024]{1,0:T(8,128)(2,1)S(1)}, bf16[176,1024]{1,0:T(8,128)(2,1)S(1)}, bf16[176,1024]{1,0:T(8,128)(2,1)S(1)}) custom-call(s32[1]{0:T(128)} %bitcast.quarter, s32[1]{0:T(128)} %get-tuple-element.93.busy, bf16[704,896]{1,0:T(8,128)(2,1)S(1)} %copy-done, bf16[704,240]{1,0:T(8,128)(2,1)S(1)} %copy-done.1, bf16[8,112,384]{2,1,0:T(8,128)(2,1)S(1)} %copy-done.3, ...), custom_call_target="tpu_custom_call" | custom-call | tf_op jit(solution)/shard_map/down/pallas_call | solution.py:517
  112.3 3.2 %collective-permute-done.24 = bf16[264,1024]{1,0:T(8,128)(2,1)S(1)} collective-permute-done((bf16[264,1024]{1,0:T(8,128)(2,1)S(1)}, bf16[264,1024]{1,0:T(8,128)(2,1)S(1)}, u32[]{:S(2)}, u32[]{:S(2)}) %collective-permute-start.24) | collective-permute-done | bytes 540704 | tf_op jit(solution)/shard_map/ppermute | solution.py:548
  115.6 2.4 %collective-permute-start.27 = (bf16[88,1024]{1,0:T(8,128)(2,1)S(1)}, bf16[88,1024]{1,0:T(8,128)(2,1)S(1)}, u32[]{:S(2)}, u32[]{:S(2)}) collective-permute-start(bf16[88,1024]{1,0:T(8,128)(2,1)S(1)} %slice.30), channel_id=1, source_target_pairs={{0,8},{1,9},{2,10},{3,11},{4,12},{5,13},{6,14},{7,15},{8,0},{9,1},... | collective-permute-start | bytes 540680 | tf_op jit(solution)/shard_map/ppermute | solution.py:548
  118.7 5.7 %collective-permute-start.29 = (bf16[88,1024]{1,0:T(8,128)(2,1)S(1)}, bf16[88,1024]{1,0:T(8,128)(2,1)S(1)}, u32[]{:S(2)}, u32[]{:S(2)}) collective-permute-start(bf16[88,1024]{1,0:T(8,128)(2,1)S(1)} %get-tuple-element.105), channel_id=1, source_target_pairs={{0,6},{1,7},{2,0},{3,1},{4,2},{5,3},{6,4},{7,5},{8,14},{9,15},{10,... | collective-permute-start | bytes 540680 | tf_op jit(solution)/shard_map/ppermute | solution.py:548
  125.0 4.2 %collective-permute-done.29 = bf16[88,1024]{1,0:T(8,128)(2,1)S(1)} collective-permute-done((bf16[88,1024]{1,0:T(8,128)(2,1)S(1)}, bf16[88,1024]{1,0:T(8,128)(2,1)S(1)}, u32[]{:S(2)}, u32[]{:S(2)}) %collective-permute-start.29) | collective-permute-done | bytes 180256 | tf_op jit(solution)/shard_map/ppermute | solution.py:548
  129.2 8.4 %collective-permute-done.31 = bf16[88,1024]{1,0:T(8,128)(2,1)S(1)} collective-permute-done((bf16[88,1024]{1,0:T(8,128)(2,1)S(1)}, bf16[88,1024]{1,0:T(8,128)(2,1)S(1)}, u32[]{:S(2)}, u32[]{:S(2)}) %collective-permute-start.31) | collective-permute-done | bytes 180256 | tf_op jit(solution)/shard_map/ppermute | solution.py:548
  (110 shorter events, 18.4 us)
Async XLA Ops:
  0.0 22.5 %collective-permute-start = (bf16[88,4096]{1,0:T(8,128)(2,1)}, bf16[88,4096]{1,0:T(8,128)(2,1)S(1)}, u32[]{:S(2)}, u32[]{:S(2)}) collective-permute-start(bf16[88,4096]{1,0:T(8,128)(2,1)} %bitcast.21), channel_id=1, source_target_pairs={{0,1},{1,0},{2,3},{3,2},{4,5},{5,4},{6,7},{7,6},{8,9},{9,8},{10,11... | collective-permute-start | bytes 2162696 | tf_op jit(solution)/shard_map/ppermute | solution.py:548
  3.2 13.9 %collective-permute-start.3 = (bf16[88,1152]{1,0:T(8,128)(2,1)S(1)}, bf16[88,1152]{1,0:T(8,128)(2,1)S(1)}, u32[]{:S(2)}, u32[]{:S(2)}) collective-permute-start(bf16[88,1152]{1,0:T(8,128)(2,1)S(1)} %concatenate.15.refs_0_), channel_id=1, source_target_pairs={{0,4},{1,5},{2,6},{3,7},{4,0},{5,1},{6,2},{7,3},{8,12},{9,13},{10,... | collective-permute-start | bytes 608264 | tf_op jit(solution)/shard_map/ppermute | solution.py:548
  6.9 10.3 %collective-permute-start.2 = (bf16[88,1152]{1,0:T(8,128)(2,1)S(1)}, bf16[88,1152]{1,0:T(8,128)(2,1)S(1)}, u32[]{:S(2)}, u32[]{:S(2)}) collective-permute-start(bf16[88,1152]{1,0:T(8,128)(2,1)S(1)} %concatenate.15.refs_0_), channel_id=1, source_target_pairs={{0,6},{1,7},{2,0},{3,1},{4,2},{5,3},{6,4},{7,5},{8,14},{9,15},{10,... | collective-permute-start | bytes 608264 | tf_op jit(solution)/shard_map/ppermute | solution.py:548
  8.2 14.3 %collective-permute-start.1 = (bf16[88,1152]{1,0:T(8,128)(2,1)S(1)}, bf16[88,1152]{1,0:T(8,128)(2,1)S(1)}, u32[]{:S(2)}, u32[]{:S(2)}) collective-permute-start(bf16[88,1152]{1,0:T(8,128)(2,1)S(1)} %concatenate.15.refs_0_), channel_id=1, source_target_pairs={{0,2},{1,3},{2,4},{3,5},{4,6},{5,7},{6,0},{7,1},{8,10},{9,11},{10,... | collective-permute-start | bytes 608264 | tf_op jit(solution)/shard_map/ppermute | solution.py:548
  25.6 8.6 %collective-permute-start.5 = (bf16[264,1024]{1,0:T(8,128)(2,1)}, bf16[264,1024]{1,0:T(8,128)(2,1)S(1)}, u32[]{:S(2)}, u32[]{:S(2)}) collective-permute-start(bf16[264,1024]{1,0:T(8,128)(2,1)} %get-tuple-element.62.rest_0_), channel_id=1, source_target_pairs={{0,1},{1,0},{2,3},{3,2},{4,5},{5,4},{6,7},{7,6},{8,9},{9,8},{10,11... | collective-permute-start | bytes 1622024 | tf_op jit(solution)/shard_map/ppermute | solution.py:548
  25.7 22.9 %collective-permute-start.7 = (bf16[264,1024]{1,0:T(8,128)(2,1)}, bf16[264,1024]{1,0:T(8,128)(2,1)S(1)}, u32[]{:S(2)}, u32[]{:S(2)}) collective-permute-start(bf16[264,1024]{1,0:T(8,128)(2,1)} %get-tuple-element.62.rest_0_), channel_id=1, source_target_pairs={{0,16},{1,17},{2,18},{3,19},{4,20},{5,21},{6,22},{7,23},{8,24},{9,... | collective-permute-start | bytes 1622024 | tf_op jit(solution)/shard_map/ppermute | solution.py:548
  27.3 21.4 %collective-permute-start.6 = (bf16[264,1024]{1,0:T(8,128)(2,1)}, bf16[264,1024]{1,0:T(8,128)(2,1)S(1)}, u32[]{:S(2)}, u32[]{:S(2)}) collective-permute-start(bf16[264,1024]{1,0:T(8,128)(2,1)} %get-tuple-element.62.rest_0_), channel_id=1, source_target_pairs={{0,8},{1,9},{2,10},{3,11},{4,12},{5,13},{6,14},{7,15},{8,0},{9,1},... | collective-permute-start | bytes 1622024 | tf_op jit(solution)/shard_map/ppermute | solution.py:548
  28.8 19.8 %collective-permute-start.9 = (bf16[88,1024]{1,0:T(8,128)(2,1)S(1)}, bf16[88,1024]{1,0:T(8,128)(2,1)S(1)}, u32[]{:S(2)}, u32[]{:S(2)}) collective-permute-start(bf16[88,1024]{1,0:T(8,128)(2,1)S(1)} %get-tuple-element.67), channel_id=1, source_target_pairs={{0,6},{1,7},{2,0},{3,1},{4,2},{5,3},{6,4},{7,5},{8,14},{9,15},{10,... | collective-permute-start | bytes 540680 | tf_op jit(solution)/shard_map/ppermute | solution.py:548
  31.5 17.1 %collective-permute-start.8 = (bf16[88,1024]{1,0:T(8,128)(2,1)S(1)}, bf16[88,1024]{1,0:T(8,128)(2,1)S(1)}, u32[]{:S(2)}, u32[]{:S(2)}) collective-permute-start(bf16[88,1024]{1,0:T(8,128)(2,1)S(1)} %get-tuple-element.67), channel_id=1, source_target_pairs={{0,2},{1,3},{2,4},{3,5},{4,6},{5,7},{6,0},{7,1},{8,10},{9,11},{10,... | collective-permute-start | bytes 540680 | tf_op jit(solution)/shard_map/ppermute | solution.py:548
  34.2 14.4 %collective-permute-start.10 = (bf16[88,1024]{1,0:T(8,128)(2,1)}, bf16[88,1024]{1,0:T(8,128)(2,1)S(1)}, u32[]{:S(2)}, u32[]{:S(2)}) collective-permute-start(bf16[88,1024]{1,0:T(8,128)(2,1)} %get-tuple-element.68), channel_id=1, source_target_pairs={{0,24},{1,25},{2,26},{3,27},{4,28},{5,29},{6,30},{7,31},{8,16},{9,... | collective-permute-start | bytes 540680 | tf_op jit(solution)/shard_map/ppermute | solution.py:548
  81.7 19.1 %collective-permute-start.18 = (bf16[352,1024]{1,0:T(8,128)(2,1)S(1)}, bf16[352,1024]{1,0:T(8,128)(2,1)S(1)}, u32[]{:S(2)}, u32[]{:S(2)}) collective-permute-start(bf16[352,1024]{1,0:T(8,128)(2,1)S(1)} %add_convert_fusion.2), channel_id=1, source_target_pairs={{0,24},{1,25},{2,26},{3,27},{4,28},{5,29},{6,30},{7,31},{8,16},{9,... | collective-permute-start | bytes 2162696 | tf_op jit(solution)/shard_map/ppermute | solution.py:548
  96.6 4.2 %collective-permute-start.19 = (bf16[176,1024]{1,0:T(8,128)(2,1)S(1)}, bf16[176,1024]{1,0:T(8,128)(2,1)S(1)}, u32[]{:S(2)}, u32[]{:S(2)}) collective-permute-start(bf16[176,1024]{1,0:T(8,128)(2,1)S(1)} %get-tuple-element.88), channel_id=1, source_target_pairs={{0,1},{1,0},{2,3},{3,2},{4,5},{5,4},{6,7},{7,6},{8,9},{9,8},{10,11... | collective-permute-start | bytes 1081352 | tf_op jit(solution)/shard_map/ppermute | solution.py:548
  96.7 4.2 %collective-permute-start.20 = (bf16[176,1024]{1,0:T(8,128)(2,1)S(1)}, bf16[176,1024]{1,0:T(8,128)(2,1)S(1)}, u32[]{:S(2)}, u32[]{:S(2)}) collective-permute-start(bf16[176,1024]{1,0:T(8,128)(2,1)S(1)} %get-tuple-element.89), channel_id=1, source_target_pairs={{0,1},{1,0},{2,3},{3,2},{4,5},{5,4},{6,7},{7,6},{8,9},{9,8},{10,11... | collective-permute-start | bytes 1081352 | tf_op jit(solution)/shard_map/ppermute | solution.py:548
  97.2 3.9 %collective-permute-start.21 = (bf16[176,1024]{1,0:T(8,128)(2,1)S(1)}, bf16[176,1024]{1,0:T(8,128)(2,1)S(1)}, u32[]{:S(2)}, u32[]{:S(2)}) collective-permute-start(bf16[176,1024]{1,0:T(8,128)(2,1)S(1)} %get-tuple-element.91), channel_id=1, source_target_pairs={{0,1},{1,0},{2,3},{3,2},{4,5},{5,4},{6,7},{7,6},{8,9},{9,8},{10,11... | collective-permute-start | bytes 1081352 | tf_op jit(solution)/shard_map/ppermute | solution.py:548
  97.3 3.9 %collective-permute-start.22 = (bf16[176,1024]{1,0:T(8,128)(2,1)S(1)}, bf16[176,1024]{1,0:T(8,128)(2,1)S(1)}, u32[]{:S(2)}, u32[]{:S(2)}) collective-permute-start(bf16[176,1024]{1,0:T(8,128)(2,1)S(1)} %get-tuple-element.92), channel_id=1, source_target_pairs={{0,1},{1,0},{2,3},{3,2},{4,5},{5,4},{6,7},{7,6},{8,9},{9,8},{10,11... | collective-permute-start | bytes 1081352 | tf_op jit(solution)/shard_map/ppermute | solution.py:548
  101.5 14.1 %collective-permute-start.24 = (bf16[264,1024]{1,0:T(8,128)(2,1)S(1)}, bf16[264,1024]{1,0:T(8,128)(2,1)S(1)}, u32[]{:S(2)}, u32[]{:S(2)}) collective-permute-start(bf16[264,1024]{1,0:T(8,128)(2,1)S(1)} %slice.28), channel_id=1, source_target_pairs={{0,16},{1,17},{2,18},{3,19},{4,20},{5,21},{6,22},{7,23},{8,24},{9,... | collective-permute-start | bytes 1622024 | tf_op jit(solution)/shard_map/ppermute | solution.py:548
  103.1 14.8 %collective-permute-start.23 = (bf16[264,1024]{1,0:T(8,128)(2,1)S(1)}, bf16[264,1024]{1,0:T(8,128)(2,1)S(1)}, u32[]{:S(2)}, u32[]{:S(2)}) collective-permute-start(bf16[264,1024]{1,0:T(8,128)(2,1)S(1)} %slice.27), channel_id=1, source_target_pairs={{0,8},{1,9},{2,10},{3,11},{4,12},{5,13},{6,14},{7,15},{8,0},{9,1},... | collective-permute-start | bytes 1622024 | tf_op jit(solution)/shard_map/ppermute | solution.py:548
  111.1 6.8 %collective-permute-start.25 = (bf16[176,1024]{1,0:T(8,128)(2,1)S(1)}, bf16[176,1024]{1,0:T(8,128)(2,1)S(1)}, u32[]{:S(2)}, u32[]{:S(2)}) collective-permute-start(bf16[176,1024]{1,0:T(8,128)(2,1)S(1)} %get-tuple-element.98), channel_id=1, source_target_pairs={{0,1},{1,0},{2,3},{3,2},{4,5},{5,4},{6,7},{7,6},{8,9},{9,8},{10,11... | collective-permute-start | bytes 1081352 | tf_op jit(solution)/shard_map/ppermute | solution.py:548
  111.2 6.7 %collective-permute-start.26 = (bf16[176,1024]{1,0:T(8,128)(2,1)S(1)}, bf16[176,1024]{1,0:T(8,128)(2,1)S(1)}, u32[]{:S(2)}, u32[]{:S(2)}) collective-permute-start(bf16[176,1024]{1,0:T(8,128)(2,1)S(1)} %get-tuple-element.99), channel_id=1, source_target_pairs={{0,1},{1,0},{2,3},{3,2},{4,5},{5,4},{6,7},{7,6},{8,9},{9,8},{10,11... | collective-permute-start | bytes 1081352 | tf_op jit(solution)/shard_map/ppermute | solution.py:548
  111.8 13.3 %collective-permute-start.28 = (bf16[88,1024]{1,0:T(8,128)(2,1)S(1)}, bf16[88,1024]{1,0:T(8,128)(2,1)S(1)}, u32[]{:S(2)}, u32[]{:S(2)}) collective-permute-start(bf16[88,1024]{1,0:T(8,128)(2,1)S(1)} %slice.31), channel_id=1, source_target_pairs={{0,16},{1,17},{2,18},{3,19},{4,20},{5,21},{6,22},{7,23},{8,24},{9,... | collective-permute-start | bytes 540680 | tf_op jit(solution)/shard_map/ppermute | solution.py:548
  115.6 9.5 %collective-permute-start.27 = (bf16[88,1024]{1,0:T(8,128)(2,1)S(1)}, bf16[88,1024]{1,0:T(8,128)(2,1)S(1)}, u32[]{:S(2)}, u32[]{:S(2)}) collective-permute-start(bf16[88,1024]{1,0:T(8,128)(2,1)S(1)} %slice.30), channel_id=1, source_target_pairs={{0,8},{1,9},{2,10},{3,11},{4,12},{5,13},{6,14},{7,15},{8,0},{9,1},... | collective-permute-start | bytes 540680 | tf_op jit(solution)/shard_map/ppermute | solution.py:548
  118.7 10.5 %collective-permute-start.29 = (bf16[88,1024]{1,0:T(8,128)(2,1)S(1)}, bf16[88,1024]{1,0:T(8,128)(2,1)S(1)}, u32[]{:S(2)}, u32[]{:S(2)}) collective-permute-start(bf16[88,1024]{1,0:T(8,128)(2,1)S(1)} %get-tuple-element.105), channel_id=1, source_target_pairs={{0,6},{1,7},{2,0},{3,1},{4,2},{5,3},{6,4},{7,5},{8,14},{9,15},{10,... | collective-permute-start | bytes 540680 | tf_op jit(solution)/shard_map/ppermute | solution.py:548
  124.4 13.2 %collective-permute-start.31 = (bf16[88,1024]{1,0:T(8,128)(2,1)S(1)}, bf16[88,1024]{1,0:T(8,128)(2,1)S(1)}, u32[]{:S(2)}, u32[]{:S(2)}) collective-permute-start(bf16[88,1024]{1,0:T(8,128)(2,1)S(1)} %get-tuple-element.106), channel_id=1, source_target_pairs={{0,4},{1,5},{2,6},{3,7},{4,0},{5,1},{6,2},{7,3},{8,12},{9,13},{10,... | collective-permute-start | bytes 540680 | tf_op jit(solution)/shard_map/ppermute | solution.py:548
  124.4 13.2 %collective-permute-start.30 = (bf16[88,1024]{1,0:T(8,128)(2,1)S(1)}, bf16[88,1024]{1,0:T(8,128)(2,1)S(1)}, u32[]{:S(2)}, u32[]{:S(2)}) collective-permute-start(bf16[88,1024]{1,0:T(8,128)(2,1)S(1)} %get-tuple-element.107), channel_id=1, source_target_pairs={{0,2},{1,3},{2,4},{3,5},{4,6},{5,7},{6,0},{7,1},{8,10},{9,11},{10,... | collective-permute-start | bytes 540680 | tf_op jit(solution)/shard_map/ppermute | solution.py:548
  (30 other events, 121.5 us)
